TPU v7x, 32 devices: a whole 2x2x4 slice. The times are simulated.
32 devices in a mesh: seq: 8 (over z, y), wshard: 4 (over x, core).
Axes of the slice: x: 2, y: 2, z: 4, core: 2. Of those that a mesh axis runs over, the one named last changes fastest.
Arguments:
- inputs: bfloat16 [4, 8192, 768], P('wshard', 'seq'), may hold values from -6 to 6
- cotangent: bfloat16 [4, 8192, 768], P('wshard', 'seq'), may hold values from -6 to 6
- lengths: int32 [4, 3], P('wshard'), may hold values from 1024 to 4096, as said below
- in_proj: bfloat16 [768, 3352], P('wshard'), may hold values from -0.21875 to 0.21875
- out_proj: bfloat16 [1536, 768], P('wshard'), may hold values from -0.15625 to 0.15625
- conv_weight: bfloat16 [4, 1792], P(None, 'wshard'), may hold values from -3 to 3
- conv_bias: bfloat16 [1792], P('wshard'), may hold values from -3 to 3
- a_log: bfloat16 [24], P('wshard'), may hold values from -1 to 2
- d_skip: bfloat16 [24], P('wshard'), may hold values from 0.5 to 1.5
- dt_bias: bfloat16 [24], P('wshard'), may hold values from -8 to -3
- norm_gain: bfloat16 [768], P('wshard'), may hold values from 0.099609375 to 1.8984375
- gate_gain: bfloat16 [1536], P('wshard'), may hold values from 0.099609375 to 1.8984375
Outputs:
- mixed: bfloat16 [4, 8192, 768], P('wshard', 'seq')
- grad_input: bfloat16 [4, 8192, 768], P('wshard', 'seq')
- grad_in_proj: float32 [768, 3352], P('wshard')
- grad_out_proj: float32 [1536, 768], P('wshard')
- grad_conv_weight: float32 [4, 1792], P(None, 'wshard')
- grad_conv_bias: float32 [1792], P('wshard')
- grad_a_log: float32 [24], P('wshard')
- grad_d_skip: float32 [24], P('wshard')
- grad_dt_bias: float32 [24], P('wshard')
- grad_norm_gain: float32 [768], P('wshard')
- grad_gate_gain: float32 [1536], P('wshard')
Inputs may be any that keep to these rules, and one draw needn't show every extreme that they name: `lengths`: each pack holds 3 documents laid end to end from position 0, each of 1024 to 4096 tokens, one exactly 4096; their sum is at most 8192, the rest is padding.
All inputs are finite; a program needn't handle non-finite values.
Results may differ from a plain program's by a relative error of at most 0.012.
Values may be sent and summed in bfloat16 or wider, within the bound.
No kernel may reach another device: no remote copies, remote signals or barrier semaphores. Data moves between devices by JAX's collectives and lax.ppermute only.
A program may use at most 256 MiB of HBM per device.

v0:
```python
import jax
import jax.numpy as jnp
from jax import lax
from jax.sharding import PartitionSpec as P

Q = 256


highest = lax.Precision.HIGHEST
eps = 1e-05


def shifted_2(value, axis, steps):
    count = lax.axis_size(axis)
    leading, last = (max(0, -steps), min(count, count - steps))
    return lax.ppermute(value, axis, [(source, source + steps) for source in range(leading, last)])


def carried_in(shard, axis, combine, identity, reverse):
    length, here = (lax.axis_size(axis), lax.axis_index(axis))
    everything = jax.tree.map(lambda part: lax.all_gather(part, axis), shard)
    start = jax.tree.map(
        lambda part, zero: jnp.broadcast_to(jnp.asarray(zero, part.dtype), part.shape),
        shard,
        identity,
    )

    def step(k, before):
        at = length - 1 - k if reverse else k
        reached = at > here if reverse else at < here
        new = combine(before, jax.tree.map(lambda part: part[at], everything))
        return jax.tree.map(lambda a, b: jnp.where(reached, a, b), new, before)

    return lax.fori_loop(0, length, step, start)


def block_terms(decay_rows, seg_rows, seg_prev):
    cum_log = jnp.cumsum(decay_rows, axis=0)
    index_line = jnp.arange(seg_rows.shape[0])
    same_doc = (seg_rows[:, None] == seg_rows[None, :]) & (
        index_line[:, None] >= index_line[None, :]
    )
    log_gap = cum_log.T[:, :, None] - cum_log.T[:, None, :]
    inside = jnp.where(same_doc[None], jnp.exp(jnp.where(same_doc[None], log_gap, 0.0)), 0.0)
    enter_decay = jnp.exp(cum_log) * (seg_rows == seg_prev).astype(jnp.float32)[:, None]
    ending = (seg_rows == seg_rows[-1]).astype(jnp.float32)[:, None] * jnp.exp(
        cum_log[-1][None, :] - cum_log
    )
    leave_decay = jnp.exp(cum_log[-1]) * (seg_rows[-1] == seg_prev).astype(jnp.float32)
    return (inside, enter_decay, ending, leave_decay)


def combine_pairs(earlier, later):
    return (earlier[0] * later[0], later[1] + later[0][:, None, None] * earlier[1])


def silu_slope(values):
    sigma = jax.nn.sigmoid(values)
    return sigma * (1.0 + values * (1.0 - sigma))


def rms_back(grad_unit, unit_rows, scale_rows):
    return scale_rows * (
        grad_unit - unit_rows * jnp.mean(grad_unit * unit_rows, axis=-1, keepdims=True)
    )


def body(
    inputs,
    cotangent,
    lengths,
    in_proj,
    out_proj,
    conv_weight,
    conv_bias,
    a_log,
    d_skip,
    dt_bias,
    norm_gain,
    gate_gain,
):
    f32 = jnp.float32
    bf16 = jnp.bfloat16
    w_in, w_out, conv_w, conv_b, log_rate, skip_coef, dt_shift, gain_in, gain_gate = (
        lax.all_gather(in_proj, "wshard", axis=0, tiled=True),
        lax.all_gather(out_proj, "wshard", axis=0, tiled=True),
        lax.all_gather(conv_weight, "wshard", axis=1, tiled=True),
        lax.all_gather(conv_bias, "wshard", axis=0, tiled=True),
        lax.all_gather(a_log, "wshard", axis=0, tiled=True),
        lax.all_gather(d_skip, "wshard", axis=0, tiled=True),
        lax.all_gather(dt_bias, "wshard", axis=0, tiled=True),
        lax.all_gather(norm_gain, "wshard", axis=0, tiled=True),
        lax.all_gather(gate_gain, "wshard", axis=0, tiled=True),
    )
    tok_rows = inputs.shape[1]
    inner_width = w_out.shape[0]
    head_count = log_rate.shape[0]
    head_dim = inner_width // head_count
    conv_width = conv_w.shape[1]
    state_dim = (conv_width - inner_width) // 2
    kernel_taps = conv_w.shape[0]
    edge_rows = kernel_taps - 1
    doc_count = lengths.shape[1]
    block_count = tok_rows // Q
    doc_ends = jnp.cumsum(lengths[0], dtype=jnp.int32)
    first_pos = lax.axis_index("seq") * tok_rows
    positions = first_pos - edge_rows + jnp.arange(tok_rows + edge_rows, dtype=jnp.int32)
    seg_ext = jnp.sum((positions[:, None] >= doc_ends[None, :]).astype(jnp.int32), axis=1)
    seg_ext = jnp.where(positions < 0, -1, seg_ext)
    segment = seg_ext[edge_rows:]
    keep_mask = (segment < doc_count).astype(f32)
    seg_before = seg_ext[edge_rows - 1 : edge_rows - 1 + tok_rows].reshape(block_count, Q)[:, 0]
    source = inputs[0].astype(f32)
    scale_in = lax.rsqrt(jnp.mean(source * source, axis=-1, keepdims=True) + eps)
    unit_in = source * scale_in
    gain_in_f = gain_in.astype(f32)
    normed = (unit_in * gain_in_f).astype(bf16)
    projected = jnp.dot(normed, w_in, preferred_element_type=f32)
    gate_in = projected[:, :inner_width]
    conv_in = projected[:, inner_width : inner_width + conv_width].astype(bf16)
    dt_raw = projected[:, inner_width + conv_width :]
    before_rows = shifted_2(conv_in[tok_rows - edge_rows :], "seq", 1)
    extended = jnp.concatenate([before_rows, conv_in], axis=0).astype(f32)
    conv_taps = conv_w.astype(f32)
    links = [
        (seg_ext[offset : offset + tok_rows] == segment).astype(f32)[:, None]
        for offset in range(kernel_taps)
    ]
    conv_pre = jnp.broadcast_to(conv_b.astype(f32), (tok_rows, conv_width))
    for offset in range(kernel_taps):
        conv_pre = (
            conv_pre + conv_taps[offset] * extended[offset : offset + tok_rows] * links[offset]
        )
    conv_out = jax.nn.silu(conv_pre)
    values_blk = conv_out[:, :inner_width].reshape(block_count, Q, head_count, head_dim)
    b_blk = conv_out[:, inner_width : inner_width + state_dim].reshape(block_count, Q, state_dim)
    c_blk = conv_out[:, inner_width + state_dim :].reshape(block_count, Q, state_dim)
    shifted = dt_raw + dt_shift.astype(f32)
    step_dt = jax.nn.softplus(shifted)
    neg_rate = -jnp.exp(log_rate.astype(f32))
    step_blk = step_dt.reshape(block_count, Q, head_count)
    decay_blk = (step_dt * neg_rate).reshape(block_count, Q, head_count)
    seg_blk = segment.reshape(block_count, Q)
    skip_f = skip_coef.astype(f32)

    def forward_block(carried, block_items):
        state_loc, kept_decay = carried
        head_values, b_rows, c_rows, decay_rows, step_rows, seg_rows, seg_prev = block_items
        inside, enter_decay, ending, leave_decay = block_terms(decay_rows, seg_rows, seg_prev)
        scores = jnp.dot(c_rows, b_rows.T, precision=highest)
        mixing = scores[None] * inside * step_rows.T[:, None, :]
        intra_out = jnp.einsum("hts,shp->thp", mixing, head_values, precision=highest)
        update = jnp.einsum(
            "shp,sn->hpn", (step_rows * ending)[:, :, None] * head_values, b_rows, precision=highest
        )
        new_state = leave_decay[:, None, None] * state_loc + update
        return (
            (new_state, kept_decay * leave_decay),
            (intra_out, state_loc, kept_decay, enter_decay),
        )

    block_items = (values_blk, b_blk, c_blk, decay_blk, step_blk, seg_blk, seg_before)
    start_carry = (jnp.zeros((head_count, head_dim, state_dim), f32), jnp.ones((head_count,), f32))
    (local_end, total_decay), (intra_all, starts_loc, decay_before, enter_all) = lax.scan(
        forward_block, start_carry, block_items
    )
    prefix_decay, incoming = carried_in(
        (total_decay, local_end),
        "seq",
        combine_pairs,
        (jnp.ones_like(total_decay), jnp.zeros_like(local_end)),
        False,
    )
    starts_full = starts_loc + decay_before[:, :, None, None] * incoming[None]
    inter_out = enter_all[..., None] * jnp.einsum(
        "ktn,khpn->kthp", c_blk, starts_full, precision=highest
    )
    ssd_blk = intra_all + inter_out + skip_f[None, None, :, None] * values_blk
    ssd_out = ssd_blk.reshape(tok_rows, inner_width)
    gate_act = jax.nn.silu(gate_in)
    gated = ssd_out * gate_act
    scale_gate = lax.rsqrt(jnp.mean(gated * gated, axis=-1, keepdims=True) + eps)
    unit_gate = gated * scale_gate
    gain_gate_f = gain_gate.astype(f32)
    gate_normed = (unit_gate * gain_gate_f).astype(bf16)
    branch = jnp.dot(gate_normed, w_out, preferred_element_type=f32)
    mixed = (keep_mask[:, None] * (source + branch)).astype(bf16)[None]
    back_in, back_out = (
        lax.all_gather(in_proj, "wshard", axis=0, tiled=True),
        lax.all_gather(out_proj, "wshard", axis=0, tiled=True),
    )
    grad_res = cotangent[0].astype(f32) * keep_mask[:, None]
    grad_branch = grad_res.astype(bf16)
    grad_w_out = jnp.einsum("ti,td->id", gate_normed, grad_branch, preferred_element_type=f32)
    grad_gnormed = jnp.einsum("td,id->ti", grad_branch, back_out, preferred_element_type=f32)
    grad_gain_gate = jnp.sum(grad_gnormed * unit_gate, axis=0)
    grad_gated = rms_back(grad_gnormed * gain_gate_f, unit_gate, scale_gate)
    grad_ssd = grad_gated * gate_act
    grad_gate_in = grad_gated * ssd_out * silu_slope(gate_in)
    grad_y = grad_ssd.reshape(block_count, Q, head_count, head_dim)
    reach = enter_all * decay_before[:, None, :]
    reach_grad = jnp.einsum("kthp,ktn->hpn", reach[..., None] * grad_y, c_blk, precision=highest)
    suffix_decay, grad_end = carried_in(
        (total_decay, reach_grad),
        "seq",
        combine_pairs,
        (jnp.ones_like(total_decay), jnp.zeros_like(reach_grad)),
        True,
    )

    def backward_block(grad_next, back_items):
        (
            head_values,
            b_rows,
            c_rows,
            decay_rows,
            step_rows,
            seg_rows,
            seg_prev,
            start_state,
            grad_out,
        ) = back_items
        inside, enter_decay, ending, leave_decay = block_terms(decay_rows, seg_rows, seg_prev)
        scores = jnp.dot(c_rows, b_rows.T, precision=highest)
        spread = step_rows.T[:, None, :]
        mixing = scores[None] * inside * spread
        weight_end = step_rows * ending
        grad_mix = jnp.einsum("thp,shp->hts", grad_out, head_values, precision=highest)
        state_read = jnp.einsum("sn,hpn->shp", b_rows, grad_next, precision=highest)
        grad_vals = (
            jnp.einsum("hts,thp->shp", mixing, grad_out, precision=highest)
            + weight_end[:, :, None] * state_read
        )
        grad_scores = jnp.sum(grad_mix * inside * spread, axis=0)
        enter_grad = enter_decay[:, :, None] * grad_out
        grad_c = jnp.dot(grad_scores, b_rows, precision=highest) + jnp.einsum(
            "thp,hpn->tn", enter_grad, start_state, precision=highest
        )
        grad_b = jnp.dot(grad_scores.T, c_rows, precision=highest) + jnp.einsum(
            "shp,hpn->sn", weight_end[:, :, None] * head_values, grad_next, precision=highest
        )
        grad_weight = jnp.sum(head_values * state_read, axis=2)
        mix_core = grad_mix * scores[None] * inside
        grad_steps = jnp.sum(mix_core, axis=1).T + grad_weight * ending
        expo = mix_core * spread
        read_prev = jnp.einsum("tn,hpn->thp", c_rows, start_state, precision=highest)
        grad_enter = jnp.sum(grad_out * read_prev, axis=2)
        end_terms = grad_weight * step_rows * ending
        grad_cum = (
            jnp.sum(expo, axis=2).T - jnp.sum(expo, axis=1).T + grad_enter * enter_decay - end_terms
        )
        grad_leave = jnp.sum(grad_next * start_state, axis=(1, 2))
        grad_cum = grad_cum.at[-1].add(grad_leave * leave_decay + jnp.sum(end_terms, axis=0))
        grad_decay = jnp.cumsum(grad_cum[::-1], axis=0)[::-1]
        grad_prev = leave_decay[:, None, None] * grad_next + jnp.einsum(
            "thp,tn->hpn", enter_grad, c_rows, precision=highest
        )
        return (grad_prev, (grad_vals, grad_b, grad_c, grad_steps, grad_decay))

    back_items = block_items + (starts_full, grad_y)
    grad_first, (grad_vals, grad_b, grad_c, grad_steps, grad_decay) = lax.scan(
        backward_block, grad_end, back_items, reverse=True
    )
    grad_values = grad_vals + skip_f[None, None, :, None] * grad_y
    grad_skip = jnp.sum(values_blk * grad_y, axis=(0, 1, 3))
    grad_step_dt = (grad_steps + grad_decay * neg_rate).reshape(tok_rows, head_count)
    grad_log_rate = jnp.sum(grad_decay.reshape(tok_rows, head_count) * step_dt, axis=0) * neg_rate
    grad_shift_in = grad_step_dt * jax.nn.sigmoid(shifted)
    grad_dt_bias = jnp.sum(grad_shift_in, axis=0)
    grad_conv_out = jnp.concatenate(
        [
            grad_values.reshape(tok_rows, inner_width),
            grad_b.reshape(tok_rows, state_dim),
            grad_c.reshape(tok_rows, state_dim),
        ],
        axis=1,
    )
    grad_pre = grad_conv_out * silu_slope(conv_pre)
    grad_conv_b = jnp.sum(grad_pre, axis=0)
    grad_conv_w = jnp.stack(
        [
            jnp.sum(grad_pre * extended[offset : offset + tok_rows] * links[offset], axis=0)
            for offset in range(kernel_taps)
        ],
        axis=0,
    )
    grad_ext = jnp.zeros((tok_rows + edge_rows, conv_width), f32)
    for offset in range(kernel_taps):
        grad_ext = grad_ext + jnp.pad(
            grad_pre * conv_taps[offset] * links[offset], ((offset, edge_rows - offset), (0, 0))
        )
    grad_edge = shifted_2(grad_ext[:edge_rows], "seq", -1)
    grad_conv_in = grad_ext[edge_rows:] + jnp.concatenate(
        [jnp.zeros((tok_rows - edge_rows, conv_width), f32), grad_edge], axis=0
    )
    grad_projected = jnp.concatenate([grad_gate_in, grad_conv_in, grad_shift_in], axis=1).astype(
        bf16
    )
    grad_w_in = jnp.einsum("td,tj->dj", normed, grad_projected, preferred_element_type=f32)
    grad_normed = jnp.einsum("tj,dj->td", grad_projected, back_in, preferred_element_type=f32)
    grad_gain_in = jnp.sum(grad_normed * unit_in, axis=0)
    grad_source = grad_res + rms_back(grad_normed * gain_in_f, unit_in, scale_in)
    grad_input = grad_source.astype(bf16)[None]
    shards = (
        lax.psum_scatter(grad_w_in, "wshard", scatter_dimension=0, tiled=True),
        lax.psum_scatter(grad_w_out, "wshard", scatter_dimension=0, tiled=True),
        lax.psum_scatter(grad_conv_w, "wshard", scatter_dimension=1, tiled=True),
        lax.psum_scatter(grad_conv_b, "wshard", scatter_dimension=0, tiled=True),
        lax.psum_scatter(grad_log_rate, "wshard", scatter_dimension=0, tiled=True),
        lax.psum_scatter(grad_skip, "wshard", scatter_dimension=0, tiled=True),
        lax.psum_scatter(grad_dt_bias, "wshard", scatter_dimension=0, tiled=True),
        lax.psum_scatter(grad_gain_in, "wshard", scatter_dimension=0, tiled=True),
        lax.psum_scatter(grad_gain_gate, "wshard", scatter_dimension=0, tiled=True),
    )
    totals = lax.psum(
        (
            shards[0],
            shards[1],
            shards[2],
            shards[3],
            shards[4],
            shards[5],
            shards[6],
            shards[7],
            shards[8],
        ),
        "seq",
    )
    return (
        mixed,
        grad_input,
        totals[0],
        totals[1],
        totals[2],
        totals[3],
        totals[4],
        totals[5],
        totals[6],
        totals[7],
        totals[8],
    )


def solution(mesh):
    placed = (
        P("wshard", "seq", None),
        P("wshard", "seq", None),
        P("wshard", None),
        P("wshard", None),
        P("wshard", None),
        P(None, "wshard"),
        P("wshard"),
        P("wshard"),
        P("wshard"),
        P("wshard"),
        P("wshard"),
        P("wshard"),
    )
    return jax.shard_map(
        body,
        mesh=mesh,
        in_specs=placed,
        out_specs=(
            P("wshard", "seq", None),
            P("wshard", "seq", None),
            P("wshard", None),
            P("wshard", None),
            P(None, "wshard"),
            P("wshard"),
            P("wshard"),
            P("wshard"),
            P("wshard"),
            P("wshard"),
            P("wshard"),
        ),
        check_vma=False,
    )
```

profile of v0, /device:TPU:0, one launch (start us, length us, event | category | flops | bytes accessed | tf_op | source)
XLA Modules:
  0.0 1196.7 jit_solution(17764460634720493918)
XLA Ops:
  33.3 20.0 %all-gather.10.cloned.1.call-done = bf16[768,3352]{1,0:T(8,128)(2,1)} async-done(((bf16[192,3352]{1,0:T(8,128)(2,1)}), bf16[768,3352]{1,0:T(8,128)(2,1)}) %all-gather.10.cloned.1.call-update) | async-done | bytes 5148688 | tf_op jit(solution)/shard_map/all_gather | solution.py:85
  53.3 11.8 fusion.178
  116.3 86.1 %while.77 = (s32[]{:T(128)}, f32[24,64,128]{2,1,0:T(8,128)S(1)}, f32[24]{0:T(128)S(1)}, f32[4,256,24,64]{1,3,2,0:T(8,128)}, f32[4,24,64,128]{3,2,1,0:T(8,128)}, ...) while((s32[]{:T(128)}, f32[24,64,128]{2,1,0:T(8,128)S(1)}, ...), condition=%wide.region_6.7_spmd.clone, body=%wide.region_3.6_spmd.clone.sunk | while | flops 1922667648 | bytes 9421095 | solution.py:164
  210.8 23.1 %all-reduce.9 = f32[192]{0:T(256)S(1)} all-reduce(f32[192]{0:T(256)S(1)} %dynamic-update-slice.13), channel_id=3, replica_groups=mesh['seq'=8,'wshard'=4] {'seq'}, use_global_device_ids=true, to_apply=%add.9 | all-reduce | flops 192 | bytes 1536
  239.2 64.7 %all-gather.14.cloned.1.call-done = f32[192,64,128]{2,1,0:T(8,128)} async-done(((f32[24,64,128]{2,1,0:T(8,128)}), f32[192,64,128]{2,1,0:T(8,128)}) %all-gather.14.cloned.1.call-update) | async-done | bytes 6291472 | tf_op jit(solution)/shard_map/all_gather | solution.py:21
  303.9 10.8 while.78
  318.7 11.2 multiply_add_fusion.2
  344.5 10.7 multiply_reduce_fusion.7
  355.2 11.7 multiply_reduce_fusion.8
  416.5 74.7 %all-gather.16.cloned.1.call-done = f32[192,64,128]{2,1,0:T(8,128)} async-done(((f32[24,64,128]{2,1,0:T(8,128)}), f32[192,64,128]{2,1,0:T(8,128)}) %all-gather.16.cloned.1.call-update) | async-done | bytes 6291472 | tf_op jit(solution)/shard_map/all_gather | solution.py:21
  491.1 11.4 while.79
  508.9 317.3 %while.76 = (s32[]{:T(128)}, f32[24,64,128]{2,1,0:T(8,128)S(1)}, f32[4,256,24,64]{1,3,2,0:T(8,128)}, f32[4,256,128]{2,1,0:T(8,128)}, f32[4,256,128]{2,1,0:T(8,12...) while((s32[]{:T(128)}, f32[24,64,128]{2,1,0:T(8,128)S(1)}, ...), condition=%wide.region_26.27_spmd, body=%wide.region_13.26_spmd.sunk | while | flops 5770691584 | bytes 31537768 | solution.py:261
  512.2 11.7 multiply_reduce_fusion.13
  591.5 11.7 multiply_reduce_fusion.13
  670.6 11.7 multiply_reduce_fusion.13
  749.8 11.7 multiply_reduce_fusion.13
  842.2 20.8 %multiply_reduce_fusion.6 = (f32[1792]{0:T(1024)S(1)}, f32[1792]{0:T(1024)S(1)}, f32[1792]{0:T(1024)S(1)}, f32[1792]{0:T(1024)S(1)}, f32[1792]{0:T(1024)S(1)}, /*index=5*/f32[1024,1792]{0,1:T(8,128)}) fusion(f32[1027,1792]{0,1:T(8,128)} %copy-done, f32[1024]{0:T(1024)S(1)} %copy-done.41, f32[1024]{0:T(1024)S(1)} %copy-done.43, f32[1024]{0:T(1024)S(1)} %copy-done.45, ...), kind=kLoop, calls=%fused_computation.182 | loop fusion | flops 40361216 | bytes 51428352 | tf_op jit(solution)/shard_map/reduce_sum | solution.py:282
  881.0 14.7 %pad_add_fusion = f32[1027,1792]{0,1:T(8,128)} fusion(f32[1024,1792]{0,1:T(8,128)} %copy-done.4, f32[1024,1792]{0,1:T(8,128)} %get-tuple-element.1098, f32[1024,1792]{0,1:T(8,128)} %get-tuple-element.1099, f32[1024,1792]{0,1:T(8,128)} %copy-done.3), kind=kLoop, calls=%fused_computation.175 | loop fusion | flops 5521152 | bytes 36721664 | tf_op jit(solution)/shard_map/add | solution.py:289
  904.2 13.9 %fusion.148 = f32[768,3352]{1,0:T(8,128)} fusion(bf16[1024,24]{0,1:T(8,128)(2,1)S(1)} %get-tuple-element.1072, bf16[1024,1792]{0,1:T(8,128)(2,1)S(1)} %fusion.127, bf16[1024,1536]{0,1:T(8,128)(2,1)S(1)} %copy-done.19, bf16[1,1024,768]{2,1,0:T(8,128)(2,1)S(1)} %copy-done.15, f32[768]{0:T(1024)S(1)} %copy-done.50, f32[1024]{0:T(1024)S(1)} %copy-done.52), kind=kOutput, calls=%fused_computation.226 | convolution fusion | flops 5295980544 | bytes 18742272 | tf_op jit(solution)/shard_map/td,tj->dj/dot_general | solution.py:299
  919.8 84.9 %reduce-scatter.6.cloned.1.call-done = f32[192,3352]{1,0:T(8,128)} async-done(((f32[768,3352]{1,0:T(8,128)}), f32[192,3352]{1,0:T(8,128)}) %reduce-scatter.6.cloned.1.call-update) | async-done | bytes 2574352 | tf_op jit(solution)/shard_map/reduce_scatter | solution.py:305
  1015.5 10.8 fusion.142
  1026.4 10.8 all-reduce.19
  1042.3 40.0 %all-reduce.17 = (f32[4,448]{1,0:T(4,128)}, f32[448]{0:T(512)}, f32[6]{0:T(128)}, f32[6]{0:T(128)}, f32[6]{0:T(128)}, /*index=5*/f32[192]{0:T(256)}, f32[384]{0:T(512)}) all-reduce(f32[4,448]{1,0:T(4,128)S(1)} %copy.295, f32[448]{0:T(512)S(1)} %dynamic-slice.16, ...), channel_id=1, replica_groups=mesh['seq'=8,'wshard'=4] {'seq'}, use_global_device_ids=true, to_apply=%region_37.38 | all-reduce | flops 2834 | bytes 22672 | tf_op jit(solution)/shard_map/psum | solution.py:315
  1082.3 101.5 %all-reduce.23.cloned.1.call-done = (f32[192,3352]{1,0:T(8,128)}, f32[384,768]{1,0:T(8,128)}) async-done(((f32[192,3352]{1,0:T(8,128)}, f32[384,768]{1,0:T(8,128)}), (f32[192,3352]{1,0:T(8,128)}, f32[384,768]{1,0:T(8,128)})) %all-reduce.23.cloned.1.call-update) | async-done | bytes 3754000 | tf_op jit(solution)/shard_map/psum | solution.py:315
  (629 shorter events, 592.0 us)
Async XLA Ops:
  7.2 46.1 %all-gather.10.cloned.1.call-start = ((), (), s32[]{:S(2)}) async-start(), calls=%async_computation.3 | async-start | bytes 6635520 | tf_op jit(solution)/shard_map/all_gather | solution.py:85
  7.9 296.0 %all-gather.14.cloned.1.call-start = ((), (), s32[]{:S(2)}) async-start(), calls=%async_computation.7 | async-start | bytes 7077888 | tf_op jit(solution)/shard_map/all_gather | solution.py:21
  31.3 51.6 %copy-start.32 = (f32[1792]{0:T(1024)}, f32[1792]{0:T(1024)S(1)}, u32[]{:S(2)}) copy-start(f32[1792]{0:T(1024)S(1)} %get-tuple-element.961) | copy-start | bytes 21508
  31.3 51.6 %copy-start.34 = (f32[1792]{0:T(1024)}, f32[1792]{0:T(1024)S(1)}, u32[]{:S(2)}) copy-start(f32[1792]{0:T(1024)S(1)} %get-tuple-element.962) | copy-start | bytes 21508
  31.3 51.6 %copy-start.36 = (f32[1792]{0:T(1024)}, f32[1792]{0:T(1024)S(1)}, u32[]{:S(2)}) copy-start(f32[1792]{0:T(1024)S(1)} %get-tuple-element.963) | copy-start | bytes 21508
  31.4 51.6 %copy-start.38 = (f32[1792]{0:T(1024)}, f32[1792]{0:T(1024)S(1)}, u32[]{:S(2)}) copy-start(f32[1792]{0:T(1024)S(1)} %get-tuple-element.964) | copy-start | bytes 21508
  33.3 375.3 %copy-start.53 = (f32[1024]{0:T(1024)}, f32[1024]{0:T(1024)S(1)}, u32[]{:S(2)}) copy-start(f32[1024]{0:T(1024)S(1)} %get-tuple-element.1103) | copy-start | bytes 12292
  65.3 13.6 %collective-permute-start = (bf16[3,1792]{0,1:T(8,128)(2,1)S(1)}, bf16[3,1792]{0,1:T(8,128)(2,1)S(1)}, u32[]{:S(2)}, u32[]{:S(2)}) collective-permute-start(bf16[3,1792]{0,1:T(8,128)(2,1)S(1)} %slice.209), channel_id=1, source_target_pairs={{0,4},{4,8},{8,12},{12,16},{16,20},{20,24},{24,28},{1,5},{5,9},{9,... | collective-permute-start | bytes 32264 | tf_op jit(solution)/shard_map/ppermute | solution.py:16
  116.3 87.9 %copy-start.66 = (u32[32]{0:T(128)S(1)}, u32[32]{0:T(128)}, u32[]{:S(2)}) copy-start(u32[32]{0:T(128)} %constant.287) | copy-start | bytes 388
  116.3 88.5 %copy-start.63 = (bf16[384]{0:T(512)(128)(2,1)S(1)}, bf16[384]{0:T(512)(128)(2,1)}, u32[]{:S(2)}) copy-start(bf16[384]{0:T(512)(128)(2,1)} %param.33) | copy-start | bytes 2308
  203.3 141.2 %all-gather.12.cloned.1.call-start = ((), (), s32[]{:S(2)}) async-start(), calls=%async_computation.4 | async-start | bytes 2949120 | tf_op jit(solution)/shard_map/all_gather | solution.py:86
  204.1 287.1 %all-gather.16.cloned.1.call-start = ((), (), s32[]{:S(2)}) async-start(), calls=%async_computation.8 | async-start | bytes 7077888 | tf_op jit(solution)/shard_map/all_gather | solution.py:21
  204.7 112.2 %copy-start.58 = (f32[24]{0:T(128)}, f32[24]{0:T(128)S(1)}, u32[]{:S(2)}) copy-start(f32[24]{0:T(128)S(1)} %convert_element_type.145) | copy-start | bytes 292
  209.9 198.7 %copy-start.46 = (f32[1536]{0:T(1024)}, f32[1536]{0:T(1024)S(1)}, u32[]{:S(2)}) copy-start(f32[1536]{0:T(1024)S(1)} %reshape.520) | copy-start | bytes 18436
  344.5 64.1 %copy-start.55 = (f32[1024]{0:T(1024)}, f32[1024]{0:T(1024)S(1)}, u32[]{:S(2)}) copy-start(f32[1024]{0:T(1024)S(1)} %add_rsqrt_fusion) | copy-start | bytes 12292
  393.6 526.2 %reduce-scatter.8.cloned.1.call-start = ((), (), s32[]{:S(2)}) async-start(), calls=%async_computation.6 | async-start | bytes 5898240 | tf_op jit(solution)/shard_map/reduce_scatter | solution.py:306
  416.4 588.3 %reduce-scatter.6.cloned.1.call-start = ((), (), s32[]{:S(2)}) async-start(), calls=%async_computation.5 | async-start | bytes 13271040 | tf_op jit(solution)/shard_map/reduce_scatter | solution.py:305
  879.6 17.2 %collective-permute-start.1 = (f32[3,1792]{1,0:T(4,128)S(1)}, f32[3,1792]{1,0:T(4,128)S(1)}, u32[]{:S(2)}, u32[]{:S(2)}) collective-permute-start(f32[3,1792]{1,0:T(4,128)S(1)} %copy.281), channel_id=1, source_target_pairs={{4,0},{8,4},{12,8},{16,12},{20,16},{24,20},{28,24},{5,1},{9,5},{13... | collective-permute-start | bytes 64520 | tf_op jit(solution)/shard_map/ppermute | solution.py:16
  918.1 89.3 %copy-start.48 = (f32[1536]{0:T(1024)S(1)}, f32[1536]{0:T(1024)}, u32[]{:S(2)}) copy-start(f32[1536]{0:T(1024)} %get-tuple-element.1073) | copy-start | bytes 18436
  918.1 89.5 %copy-start.47 = (f32[1536]{0:T(1024)S(1)}, f32[1536]{0:T(1024)}, u32[]{:S(2)}) copy-start(f32[1536]{0:T(1024)} %copy-done.46) | copy-start | bytes 18436
  918.1 89.5 %copy-start.54 = (f32[1024]{0:T(1024)S(1)}, f32[1024]{0:T(1024)}, u32[]{:S(2)}) copy-start(f32[1024]{0:T(1024)} %copy-done.53) | copy-start | bytes 12292
  918.1 89.5 %copy-start.56 = (f32[1024]{0:T(1024)S(1)}, f32[1024]{0:T(1024)}, u32[]{:S(2)}) copy-start(f32[1024]{0:T(1024)} %copy-done.55) | copy-start | bytes 12292
  918.1 123.1 %reduce-scatter.10.cloned.1.call-start = ((), (), s32[]{:S(2)}) async-start(), calls=%async_computation.9 | async-start | bytes 1146880
  919.5 264.3 %all-reduce.23.cloned.1.call-start = ((), (), s32[]{:S(2)}) async-start(), calls=%async_computation.10 | async-start | bytes 7667712 | tf_op jit(solution)/shard_map/psum | solution.py:315
  (73 other events, 1037.7 us)
Sparse Core Ops, SparseCore 0:
  9.6 43.6 all-gather.9
  203.4 100.3 all-gather.13
  305.4 22.2 all-gather.11
  393.7 97.3 all-gather.15
  493.5 46.0 reduce-scatter.7
  918.2 86.4 reduce-scatter.5
  1008.1 24.2 reduce-scatter.9
  1036.0 147.7 all-reduce.22
where the time goes:
time: 1210 us; the launch traced here: 1200 us
  waiting for transfers between devices  353 us (29%)
  matrix products  302 us (25%)
  local copies, waits for them, and re-layouts  222 us (18%)
  other arithmetic  189 us (16%)
  blocking collectives  92.9 us (8%)
  between operations  20.7 us (2%)
  loops' own time  12.1 us (1%)
    all_gather x2, waiting for transfers between devices, carried_in(): everything = jax.tree.map(lambda part: lax.all_gather(part, axis), shard)  139 us
    psum x1, waiting for transfers between devices, body(): lax.psum((shards[0], shards[1], shards[2], shards[3], shards[4], shards[5...  102 us
    reduce_scatter x1, waiting for transfers between devices, body(): lax.psum_scatter(grad_w_in, 'wshard', scatter_dimension=0, tiled=True)  84.9 us
    dot_general x4, matrix products, backward_block(): jnp.einsum('thp,shp->hts', grad_out, head_values, precision=highest)  46.6 us
    unnamed x157, local copies, waits for them, and re-layouts  45.7 us
    unnamed x3, blocking collectives  42.5 us
    psum x1, blocking collectives, body(): lax.psum((shards[0], shards[1], shards[2], shards[3], shards[4], shards[5...  40 us
    dot_general x4, matrix products, forward_block(): jnp.einsum('hts,shp->thp', mixing, head_values, precision=highest)  38.3 us
  transfers between devices with their start and end apart: 10, of which 6 were waited for; matrix products, arithmetic and copies ran while one was open for 43% of the time, Pallas kernels for 0%

commit v1 on v0

v1 whole, which is shorter than its diff:
```python
import jax
import jax.numpy as jnp
from jax import lax
from jax.experimental import pallas as pl
from jax.experimental.pallas import tpu as pltpu
from jax.sharding import PartitionSpec as P

f32 = jnp.float32
bf16 = jnp.bfloat16
EPS = 1e-05
LOG2E = 1.4426950408889634
CH = 128
TB = 256
LONGEST = 4096
HIGH = lax.Precision.HIGHEST
VMEM = 60 * 1024 * 1024


def sigmoid(v):
    return 0.5 * jnp.tanh(0.5 * v) + 0.5


def dot(a, b):
    return jnp.dot(a, b, preferred_element_type=f32)


def dot_nt(a, b):
    return lax.dot_general(a, b, (((1,), (1,)), ((), ())), preferred_element_type=f32)


def two(v):
    hi = v.astype(bf16)
    return hi, (v - hi.astype(f32)).astype(bf16)


def spread(v, e2):
    return dot(jnp.concatenate(two(v), axis=1), e2)


def cost(us):
    return pl.CostEstimate(flops=int(us * 1.1e9), bytes_accessed=1 << 20, transcendentals=0)


def call(kernel, grid, ins, outs, scratch, us, args, name):
    return pl.pallas_call(
        kernel,
        grid_spec=pltpu.PrefetchScalarGridSpec(
            num_scalar_prefetch=1,
            grid=grid,
            in_specs=ins,
            out_specs=[o[0] for o in outs],
            scratch_shapes=scratch,
        ),
        out_shape=[jax.ShapeDtypeStruct(o[1], o[2]) for o in outs],
        compiler_params=pltpu.CompilerParams(
            vmem_limit_bytes=VMEM, dimension_semantics=("arbitrary",)
        ),
        cost_estimate=cost(us),
        name=name,
    )(*args)


def rows(block, cols, col=0):
    return pl.BlockSpec((block, cols), lambda i, s: (i, col))


def whole(shape):
    return pl.BlockSpec(shape, lambda i, s: (0,) * len(shape))


def norm_rows(uf, gain):
    scale = lax.rsqrt(jnp.mean(uf * uf, axis=-1, keepdims=True) + EPS)
    return (uf * scale * gain).astype(bf16)


def place(buf, ids, parts, width):
    for j, part in enumerate(parts):
        n = part.shape[0]
        at = pl.multiple_of(ids[j] * n, 64)
        buf[pl.ds(at, n), :width] = part[...]


def front_kernel(np_, di, conv, heads):
    def kernel(ids, u, ue, gain, *rest):
        parts = rest[:np_]
        (cw, cb, dtb, nr, tok, e2, nrm_o, xbc_o, xc_o, slope_o, xd_o, dts_o, cc_o, ct_o,
         st_o, db_o, end_o, tot_o, nrme_o, xbce_o, wbuf, ext, state, kd, sp) = rest[np_:]
        i = pl.program_id(0)
        n = (conv - di) // 2

        @pl.when(i == 0)
        def _():
            wbuf[:, conv:] = jnp.zeros((wbuf.shape[0], wbuf.shape[1] - conv), bf16)
            place(wbuf, ids, parts, conv + heads)
            nrme = norm_rows(ue[...].astype(f32), gain[...])
            nrme_o[...] = nrme
            pe = dot(nrme, wbuf[:, :conv]).astype(bf16)
            xbce_o[...] = pe
            ext[0:8, :] = pe.astype(f32)[8:16]
            state[...] = jnp.zeros_like(state)
            kd[...] = jnp.ones_like(kd)

        nrm = norm_rows(u[...].astype(f32), gain[...])
        nrm_o[...] = nrm
        pd = dot(nrm, wbuf[:, conv:])
        for c0 in range(0, conv, 256):
            px = dot(nrm, wbuf[:, c0 : c0 + 256]).astype(bf16)
            xbc_o[:, c0 : c0 + 256] = px
            ext[8 : 8 + TB, c0 : c0 + 256] = px.astype(f32)
        sh = pd + dtb[...]
        dt = jnp.maximum(sh, 0.0) + jnp.log1p(jnp.exp(-jnp.abs(sh)))
        dts_o[:, :128] = dt
        dts_o[:, 128:] = jax.nn.sigmoid(sh)
        a2 = dt * nr[...]
        ri = lax.broadcasted_iota(jnp.int32, (CH, CH), 0)
        ci = lax.broadcasted_iota(jnp.int32, (CH, CH), 1)
        low = (ri >= ci).astype(f32)
        pieces = [dt]
        leaves = []
        for k in range(TB // CH):
            r = slice(k * CH, (k + 1) * CH)
            c2 = jnp.dot(low, a2[r], precision=HIGH, preferred_element_type=f32)
            cc_o[r, :] = c2
            ct_o[:, r] = c2.T[: ct_o.shape[0], :]
            pieces.append(jnp.exp2(c2[CH - 1 :] - c2) * tok[r, 2:3])
            leaves.append(jnp.exp2(c2[CH - 1 :]) * tok[(k + 1) * CH - 1 : (k + 1) * CH, 1:2])
        lv = jnp.concatenate([jnp.broadcast_to(v, (8, 128)) for v in leaves], axis=0)
        sp[...] = spread(jnp.concatenate(pieces + [lv], axis=0), e2[...])
        for r0 in range(0, TB, 64):
            l0, l1, l2 = tok[r0 : r0 + 64, 3:4], tok[r0 : r0 + 64, 4:5], tok[r0 : r0 + 64, 5:6]
            for c0 in range(0, conv, 256):
                c = slice(c0, c0 + 256)
                pre = cb[:, c] + cw[3:4, c] * ext[8 + r0 : 72 + r0, c]
                pre = pre + cw[2:3, c] * (ext[7 + r0 : 71 + r0, c] * l2)
                pre = pre + cw[1:2, c] * (ext[6 + r0 : 70 + r0, c] * l1)
                pre = pre + cw[0:1, c] * (ext[5 + r0 : 69 + r0, c] * l0)
                sg = sigmoid(pre)
                xc = pre * sg
                xc_o[r0 : r0 + 64, c] = xc.astype(bf16)
                slope_o[r0 : r0 + 64, c] = (sg + xc * (1.0 - sg)).astype(bf16)
                if c0 < di:
                    xd_o[r0 : r0 + 64, c] = (xc * sp[r0 : r0 + 64, c]).astype(bf16)
        ext[0:8, :] = ext[TB : TB + 8, :]
        for k in range(TB // CH):
            r = slice(k * CH, (k + 1) * CH)
            st_o[k] = state[...].astype(bf16)
            db_o[k] = jnp.broadcast_to(kd[...], (8, 128))
            bt = xc_o[r, di : di + n].astype(f32).T.astype(bf16)
            for c0 in range(0, di, 256):
                c = slice(c0, c0 + 256)
                xw = (xd_o[r, c].astype(f32) * sp[TB + k * CH : TB + (k + 1) * CH, c]).astype(bf16)
                lvr = sp[2 * TB + 8 * k : 2 * TB + 8 * k + 1, c]
                state[:, c] = lvr * state[:, c] + dot(bt, xw)
            kd[...] = kd[...] * leaves[k]

        @pl.when(i == pl.num_programs(0) - 1)
        def _():
            end_o[...] = state[...]
            tot_o[...] = spread(jnp.broadcast_to(kd[...], (8, 128)), e2[...])

    return kernel


def inner_kernel(heads, di):
    p = di // heads
    per = 128 // p

    def kernel(ids, b, c, xd, cc, ct, tok, segr, y_o):
        s = dot_nt(c[...], b[...])
        ri = lax.broadcasted_iota(jnp.int32, (CH, CH), 0)
        ci = lax.broadcasted_iota(jnp.int32, (CH, CH), 1)
        bias = jnp.where((tok[:, 0:1] == segr[...]) & (ri >= ci), 0.0, -1e30)
        lanes = lax.broadcasted_iota(jnp.int32, (1, 128), 1) // p
        for j in range(heads // per):
            xp = xd[:, 128 * j : 128 * j + 128]
            ms, xs = [], []
            for q in range(per):
                h = per * j + q
                e = jnp.exp2(cc[:, h : h + 1] - ct[h : h + 1, :] + bias)
                ms.append((s * e).astype(bf16))
                xs.append(xp * (lanes == q).astype(f32).astype(bf16))
            out = dot(jnp.concatenate(ms, axis=1), jnp.concatenate(xs, axis=0))
            y_o[:, 128 * j : 128 * j + 128] = out.astype(bf16)

    return kernel


def gate_kernel(np_, di, d):
    def kernel(ids, nrm, yin, x, c_in, cc, tok, st, db, inc, u, cot, *rest):
        wz, wo = rest[:np_], rest[np_ : 2 * np_]
        (gain, dsk, e2, mixed_o, gn_o, dz_o, dy_o, edy_o, e_o, sf_o, dc_o, rin_o, gg_o, gs_o,
         rg_o, zbuf, obuf, z, yi, dgn, ee, pr) = rest[2 * np_ :]
        i = pl.program_id(0)

        @pl.when(i == 0)
        def _():
            place(zbuf, ids, wz, di)
            place(obuf, ids, wo, d)
            gg_o[...] = jnp.zeros_like(gg_o)
            gs_o[...] = jnp.zeros_like(gs_o)
            rg_o[...] = jnp.zeros_like(rg_o)

        keep = tok[:, 6:7]
        ef = cot[...].astype(f32) * keep
        e = ef.astype(bf16)
        e_o[...] = e
        nb = TB // CH
        ents = []
        for k in range(nb):
            r = slice(k * CH, (k + 1) * CH)
            ents.append(jnp.exp2(cc[r, :]) * tok[r, 1:2])
        ee[...] = spread(jnp.concatenate(ents + [db[k] for k in range(nb)], axis=0), e2[...])
        for k in range(nb):
            r = slice(k * CH, (k + 1) * CH)
            for c0 in range(0, di, 256):
                c = slice(c0, c0 + 256)
                dbr = ee[TB + 8 * k : TB + 8 * k + 1, c]
                sf = (st[k, :, c].astype(f32) + dbr * inc[:, c].astype(f32)).astype(bf16)
                sf_o[k, :, c] = sf
                yi[r, c] = dot(c_in[r, :], sf)
        z[...] = dot(nrm[...], zbuf[...])
        dgn[...] = dot_nt(e, obuf[...])

        def strip(t, carry):
            r = pl.ds(pl.multiple_of(t * 16, 16), 16)
            xs = x[r, :].astype(f32)
            eyi = ee[r, :] * yi[r, :]
            y = yin[r, :].astype(f32) + eyi + dsk[...] * xs
            zz = z[r, :]
            sg = sigmoid(zz)
            act = zz * sg
            g = y * act
            scale = lax.rsqrt(jnp.mean(g * g, axis=-1, keepdims=True) + EPS)
            ug = g * scale
            gn_o[r, :] = (ug * gain[...]).astype(bf16)
            dg0 = dgn[r, :]
            pg = dg0 * ug
            gg_o[...] += pg[0:8] + pg[8:16]
            dn = dg0 * gain[...]
            m = jnp.mean(dn * ug, axis=-1, keepdims=True)
            dg = scale * (dn - ug * m)
            dy = dg * act
            dz_o[r, :] = (dg * y * (sg + act * (1.0 - sg))).astype(bf16)
            dy_o[r, :] = dy.astype(bf16)
            ps = xs * dy
            gs_o[...] += ps[0:8] + ps[8:16]
            edy_o[r, :] = (dy * ee[r, :]).astype(bf16)
            pr[r, :] = (dy * eyi).astype(bf16)
            return carry

        lax.fori_loop(0, TB // 16, strip, 0)
        rin_o[...] = dot_nt(pr[...], e2[0:128, :])
        mixed_o[...] = (keep * (u[...].astype(f32) + dot(gn_o[...], obuf[...]))).astype(bf16)
        for k in range(nb):
            r = slice(k * CH, (k + 1) * CH)
            ctr = c_in[r, :].astype(f32).T.astype(bf16)
            for c0 in range(0, di, 256):
                c = slice(c0, c0 + 256)
                dcv = dot(ctr, edy_o[r, c])
                dc_o[k, :, c] = dcv
                rg_o[:, c] += ee[TB + 8 * k : TB + 8 * k + 1, c] * dcv

    return kernel


def inner_back_kernel(heads, di):
    p = di // heads
    per = 128 // p

    def kernel(ids, b, c, xd, dy, cc, ct, tok, segr, gxd_o, db_o, dc_o, rk_o, gs, rr):
        st = dot_nt(b[...], c[...])
        si = lax.broadcasted_iota(jnp.int32, (CH, CH), 0)
        ti = lax.broadcasted_iota(jnp.int32, (CH, CH), 1)
        bias = jnp.where((tok[:, 0:1] == segr[...]) & (ti >= si), 0.0, -1e30)
        lanes = lax.broadcasted_iota(jnp.int32, (1, 128), 1) // p
        rr[...] = jnp.zeros_like(rr)
        rk_o[...] = jnp.zeros_like(rk_o)
        gsum = jnp.zeros((CH, CH), f32)
        for j in range(heads // per):
            xp = xd[:, 128 * j : 128 * j + 128]
            dyp = dy[:, 128 * j : 128 * j + 128]
            dys = jnp.concatenate(
                [dyp * (lanes == q).astype(f32).astype(bf16) for q in range(per)], axis=0
            )
            gm = dot_nt(xp, dys)
            ms = []
            for q in range(per):
                h = per * j + q
                e = jnp.exp2(ct[h : h + 1, :] - cc[:, h : h + 1] + bias)
                ms.append((st * e).astype(bf16))
                ge = gm[:, q * CH : (q + 1) * CH] * e
                gsum = gsum + ge
                ex = ge * st
                rr[h : h + 1, :] = jnp.sum(ex, axis=0, keepdims=True)
                rk_o[:, h : h + 1] = jnp.sum(ex, axis=1, keepdims=True)
            out = dot(jnp.concatenate(ms, axis=1), dys)
            gxd_o[:, 128 * j : 128 * j + 128] = out.astype(bf16)
        rk_o[...] = rr[...].T - rk_o[...]
        db_o[...] = dot(gsum.astype(bf16), c[...])
        dc_o[...] = dot(gsum.T.astype(bf16), b[...])

    return kernel


def back_kernel(di, conv, heads):
    def kernel(ids, xc, b_in, slope, xbc, xbce, xd, dts, cc, tok, elink, gxd, dbi, dci, rk, rin, dy, edy,
               sf, dcs, gend, cw, dsk, nr, e2, gp_o, edge_o, gw_o, gb_o, ga_o, gdt_o,
               ds, sp, sr, ext, xw, xq, xe):
        i = pl.program_id(0)
        n = (conv - di) // 2
        nb = TB // CH

        @pl.when(i == 0)
        def _():
            ds[...] = gend[...].astype(f32)
            ext[TB : TB + 8, :] = jnp.zeros((8, conv), f32)
            gw_o[...] = jnp.zeros_like(gw_o)
            gb_o[...] = jnp.zeros_like(gb_o)
            ga_o[...] = jnp.zeros_like(ga_o)
            gdt_o[...] = jnp.zeros_like(gdt_o)

        dt = dts[:, :128]
        pieces, leaves = [dt], []
        for k in range(nb):
            r = slice(k * CH, (k + 1) * CH)
            c2 = cc[r, :]
            pieces.append(jnp.exp2(c2[CH - 1 :] - c2) * tok[r, 2:3])
            leaves.append(jnp.exp2(c2[CH - 1 :]) * tok[(k + 1) * CH - 1 : (k + 1) * CH, 1:2])
        lv = jnp.concatenate([jnp.broadcast_to(v, (8, 128)) for v in leaves], axis=0)
        sp[...] = spread(jnp.concatenate(pieces + [lv], axis=0), e2[...])
        lsum = [None] * nb
        for k in reversed(range(nb)):
            r = slice(k * CH, (k + 1) * CH)
            lacc = []
            gb = dbi[r, :]
            gc = dci[r, :]
            for c0 in range(0, di, 256):
                c = slice(c0, c0 + 256)
                dsv = ds[:, c]
                dsb = dsv.astype(bf16)
                sfv = sf[k, :, c]
                sr[r, c] = dot(b_in[r, :], dsb)
                xwv = (xd[r, c].astype(f32) * sp[TB + k * CH : TB + (k + 1) * CH, c]).astype(bf16)
                gb = gb + dot_nt(xwv, dsb)
                gc = gc + dot_nt(edy[r, c], sfv)
                lacc.append(jnp.sum(dsv * sfv.astype(f32), axis=0, keepdims=True))
                lvr = sp[2 * TB + 8 * k : 2 * TB + 8 * k + 1, c]
                ds[:, c] = lvr * dsv + dcs[k, :, c]
            lrow = jnp.broadcast_to(jnp.concatenate(lacc, axis=1), (8, di))
            lhi, llo = two(lrow)
            lsum[k] = (dot_nt(lhi, e2[0:128, :]) + dot_nt(llo, e2[0:128, :]))[0:1]
            ext[r, di : di + n] = gb * slope[r, di : di + n].astype(f32)
            ext[r, di + n :] = gc * slope[r, di + n :].astype(f32)

        def strip(t, carry):
            r = pl.ds(pl.multiple_of(t * 16, 16), 16)
            re = pl.ds(pl.multiple_of(TB + t * 16, 16), 16)
            x = xc[r, :].astype(f32)
            es = sp[re, :] * sr[r, :]
            q = gxd[r, :].astype(f32) + es
            gx = sp[r, :] * q + dsk[...] * dy[r, :].astype(f32)
            ext[r, 0:di] = gx * slope[r, 0:di].astype(f32)
            xq[r, :] = (x * q).astype(bf16)
            xe[r, :] = (x * es).astype(bf16)
            return carry

        lax.fori_loop(0, TB // 16, strip, 0)
        gdt = dot_nt(xq[...], e2[0:128, :])
        et = dot_nt(xe[...], e2[0:128, :]) * dt
        ri = lax.broadcasted_iota(jnp.int32, (CH, CH), 0)
        ci = lax.broadcasted_iota(jnp.int32, (CH, CH), 1)
        tri = jnp.concatenate([(ci >= ri).astype(f32), (ci < ri).astype(f32)], axis=1)
        for k in range(nb):
            r = slice(k * CH, (k + 1) * CH)
            v = jnp.concatenate([rk[r, :] + rin[r, :], et[r]], axis=0)
            ga = jnp.dot(tri, v, precision=HIGH, preferred_element_type=f32) + lsum[k] * leaves[k]
            dtk = dts[r, :128]
            ddt = (gdt[r] + ga * nr[...]) * dts[r, 128:]
            gad = ga * dtk
            acc_a, acc_d = gad[0:8], ddt[0:8]
            for q in range(8, CH, 8):
                acc_a = acc_a + gad[q : q + 8]
                acc_d = acc_d + ddt[q : q + 8]
            ga_o[...] += acc_a
            gdt_o[...] += acc_d
            gp_o[r, conv:] = ddt.astype(bf16)
        for r0 in range(0, TB, 64):
            for c0 in range(0, conv, 256):
                c = slice(c0, c0 + 256)
                g0 = ext[r0 : r0 + 64, c]
                xb = xbc[r0 : r0 + 64, c].astype(f32)
                gsum = cw[3:4, c] * g0
                ws = [None, None, None, g0 * xb]
                for s in (1, 2, 3):
                    gs = ext[r0 + s : r0 + s + 64, c] * tok[r0 : r0 + 64, 6 + s : 7 + s]
                    gsum = gsum + cw[3 - s : 4 - s, c] * gs
                    ws[3 - s] = gs * xb
                gp_o[r0 : r0 + 64, c] = gsum.astype(bf16)
                gb = g0[0:8]
                for q in range(8, 64, 8):
                    gb = gb + g0[q : q + 8]
                gb_o[:, c] += gb
                for o in range(4):
                    w = ws[o][0:8]
                    for q in range(8, 64, 8):
                        w = w + ws[o][q : q + 8]
                    gw_o[8 * o : 8 * o + 8, c] += w
        ext[TB : TB + 8, :] = ext[0:8, :]

        @pl.when(i == pl.num_programs(0) - 1)
        def _():
            zero = jnp.zeros((8, 256), f32)
            for c0 in range(0, conv, 256):
                c = slice(c0, c0 + 256)
                xb = xbce[8:16, c].astype(f32)
                ext[8:16, c] = ext[TB : TB + 8, c]
                ext[0:8, c] = zero
                gsum = zero
                for s in (1, 2, 3):
                    gs = ext[s : s + 8, c] * elink[:, 6 + s : 7 + s]
                    gsum = gsum + cw[3 - s : 4 - s, c] * gs
                    gw_o[8 * (3 - s) : 8 * (3 - s) + 8, c] += gs * xb
                edge_o[:, c] = jnp.concatenate([zero, gsum], axis=0).astype(bf16)

    return kernel


def input_kernel(np_, di, conv, heads):
    def kernel(ids, gpz, gpx, edge, u, e, *rest):
        wz, wx = rest[:np_], rest[np_ : 2 * np_]
        gain, gi_o, gg_o, zbuf, xbuf = rest[2 * np_ :]
        i = pl.program_id(0)

        @pl.when(i == 0)
        def _():
            xbuf[:, conv:] = jnp.zeros((xbuf.shape[0], xbuf.shape[1] - conv), bf16)
            place(zbuf, ids, wz, di)
            place(xbuf, ids, wx, conv + heads)
            gg_o[...] = jnp.zeros_like(gg_o)

        gn = dot_nt(gpz[...], zbuf[...]) + dot_nt(gpx[...], xbuf[...])
        last = (i == pl.num_programs(0) - 1).astype(f32)
        tail = dot_nt(edge[...], xbuf[:, :conv]) * last
        gn = jnp.concatenate([gn[: TB - 16], gn[TB - 16 :] + tail], axis=0)
        uf = u[...].astype(f32)
        scale = lax.rsqrt(jnp.mean(uf * uf, axis=-1, keepdims=True) + EPS)
        unit = uf * scale
        pg = gn * unit
        acc = pg[0:8]
        for q in range(8, TB, 8):
            acc = acc + pg[q : q + 8]
        gg_o[...] += acc
        dn = gn * gain[...]
        m = jnp.mean(dn * unit, axis=-1, keepdims=True)
        gi_o[...] = (e[...].astype(f32) + scale * (dn - unit * m)).astype(bf16)

    return kernel


def swap(v, axis, bit):
    return lax.ppermute(v, axis, [(k, k ^ bit) for k in range(lax.axis_size(axis))])


def shift(v, axis, steps):
    n = lax.axis_size(axis)
    return lax.ppermute(v, axis, [(k, k + steps) for k in range(n) if 0 <= k + steps < n])


def bits_of(n):
    return [1 << k for k in reversed(range((n - 1).bit_length()))]


def gather_parts(v, axis):
    parts = [v]
    for bit in bits_of(lax.axis_size(axis)):
        parts = parts + [swap(p, axis, bit) for p in parts]
    return parts


def part_ids(axis):
    ids = [lax.axis_index(axis)]
    for bit in bits_of(lax.axis_size(axis)):
        ids = ids + [k ^ bit for k in ids]
    return ids


def halve(v, axis, bit, at):
    send = lax.dynamic_index_in_dim(v, 1 - at, 0, keepdims=False)
    mine = lax.dynamic_index_in_dim(v, at, 0, keepdims=False)
    got = swap(send, axis, bit)
    return (mine.astype(f32) + got.astype(f32)).astype(bf16)


def reduce_rows(g):
    nw, ns = lax.axis_size("wshard"), lax.axis_size("seq")
    w, s = lax.axis_index("wshard"), lax.axis_index("seq")
    cols = g.shape[1]
    v = g.reshape(nw, -1, cols)
    bit = 1
    while bit < nw:
        v = v.reshape(-1, 2, v.shape[-2], cols).swapaxes(0, 1)
        v = halve(v, "wshard", bit, (w // bit) % 2)
        bit *= 2
    v = v.reshape(-1, cols)
    n = v.shape[0]
    for bit in [1 << k for k in range((ns - 1).bit_length())]:
        v = halve(v.reshape(2, -1, cols), "seq", bit, (s // bit) % 2)
    for bit in bits_of(ns):
        got = swap(v, "seq", bit)
        first = (s // bit) % 2 == 0
        v = jnp.concatenate([jnp.where(first, v, got), jnp.where(first, got, v)], axis=0)
    return v.astype(f32)


def pack_state(decay, state):
    hi, lo = two(decay)
    return jnp.concatenate([state.astype(bf16), hi, lo], axis=0)


def unpack_state(v, n):
    return v[n : n + 8].astype(f32)[:1] + v[n + 8 : n + 16].astype(f32)[:1], v[:n].astype(f32)


def carried(decay, state, sign):
    n = state.shape[0]
    tokens = carried_tokens[0]
    span = 1
    while span < -(-LONGEST // tokens):
        d, s = unpack_state(shift(pack_state(decay, state), "seq", sign * span), n)
        state = state + decay[:1] * s
        decay = decay * d
        span *= 2
    return shift(state.astype(bf16), "seq", sign)


carried_tokens = [1024]


def body(inputs, cotangent, lengths, in_proj, out_proj, conv_weight, conv_bias, a_log, d_skip,
         dt_bias, norm_gain, gate_gain):
    t, d = inputs.shape[1:]
    nw = lax.axis_size("wshard")
    di = out_proj.shape[0] * nw
    heads = a_log.shape[0] * nw
    conv = conv_bias.shape[0] * nw
    taps = conv_weight.shape[0]
    n = (conv - di) // 2
    p = di // heads
    docs = lengths.shape[1]
    nt, nc, nb = t // TB, t // CH, TB // CH
    wide = conv + 128
    carried_tokens[0] = t
    wx, wz = in_proj[:, di:], in_proj[:, :di]
    wx_parts = gather_parts(wx, "wshard")
    wz_parts = gather_parts(wz, "wshard")
    wo_parts = gather_parts(out_proj, "wshard")
    ids = jnp.stack(part_ids("wshard")).astype(jnp.int32)
    small = jnp.concatenate(
        [conv_weight.reshape(-1), conv_bias, a_log, d_skip, dt_bias, norm_gain, gate_gain]
    )[None]
    small = lax.all_gather(small, "wshard", axis=0, tiled=True).astype(f32)
    sizes = [taps * conv // nw, conv // nw, heads // nw, heads // nw, heads // nw, d // nw, di // nw]
    cut, off = [], 0
    for k in sizes:
        cut.append(small[:, off : off + k])
        off += k
    cw = cut[0].reshape(nw, taps, conv // nw).swapaxes(0, 1).reshape(taps, conv)
    cb, log_rate, skip, dtb, gain_in, gain_gate = [v.reshape(1, -1) for v in cut[1:]]
    rate = -jnp.exp(log_rate)
    pad = ((0, 0), (0, 128 - heads))
    nr = jnp.pad(rate, pad)
    nr2 = nr * LOG2E
    dtb = jnp.pad(dtb, pad)
    dsk = jnp.repeat(skip, p, axis=1)
    head_of = jnp.arange(di, dtype=jnp.int32) // p
    e1 = (jnp.arange(128, dtype=jnp.int32)[:, None] == head_of[None]).astype(bf16)
    e2 = jnp.concatenate([e1, e1], axis=0)
    first = lax.axis_index("seq") * t
    pos = first - 8 + jnp.arange(t + 16, dtype=jnp.int32)
    ends = jnp.cumsum(lengths[0], dtype=jnp.int32)
    seg = jnp.sum((pos[:, None] >= ends[None]).astype(jnp.int32), axis=1)
    seg = jnp.where(pos < 0, -1, seg)
    here = seg[: t + 8]
    own = seg[8 : t + 8]
    entering = jnp.repeat(seg[7 : t + 7 : CH], CH)
    leaving = jnp.repeat(seg[7 + CH : t + 8 : CH], CH)
    zero8 = jnp.zeros((8,), jnp.int32)
    back = [jnp.concatenate([zero8, (seg[8 - k : t + 8 - k] == own).astype(jnp.int32)]) for k in (3, 2, 1)]
    ahead = [(seg[k : t + 8 + k] == here).astype(jnp.int32) for k in (1, 2, 3)]
    cols = [here, jnp.concatenate([zero8, (entering == own).astype(jnp.int32)]),
            jnp.concatenate([zero8, (leaving == own).astype(jnp.int32)])]
    cols = cols + back + [(here < docs).astype(jnp.int32)] + ahead + [jnp.zeros_like(here)] * 6
    tok_all = jnp.stack(cols, axis=1).astype(f32)
    tok, elink = tok_all[8:], tok_all[:8]
    segr = own.astype(f32)[None]
    u, cot = inputs[0], cotangent[0]
    ue = shift(u[t - 16 :], "seq", 1)

    outs = [
        (rows(TB, d), (t, d), bf16),
        (rows(TB, conv), (t, conv), bf16),
        (rows(TB, conv), (t, conv), bf16),
        (rows(TB, conv), (t, conv), bf16),
        (rows(TB, di), (t, di), bf16),
        (rows(TB, 256), (t, 256), f32),
        (rows(TB, 128), (t, 128), f32),
        (pl.BlockSpec((32, TB), lambda i, s: (0, i)), (32, t), f32),
        (pl.BlockSpec((nb, n, di), lambda i, s: (i, 0, 0)), (nc, n, di), bf16),
        (pl.BlockSpec((nb, 8, 128), lambda i, s: (i, 0, 0)), (nc, 8, 128), f32),
        (whole((n, di)), (n, di), f32),
        (whole((8, di)), (8, di), f32),
        (whole((16, d)), (16, d), bf16),
        (whole((16, conv)), (16, conv), bf16),
    ]
    ins = [rows(TB, d), whole((16, d)), whole((1, d))] + [whole(v.shape) for v in wx_parts]
    ins += [whole((taps, conv)), whole((1, conv)), whole((1, 128)), whole((1, 128)), rows(TB, 16), whole((256, di))]
    scratch = [
        pltpu.VMEM((d, wide), bf16),
        pltpu.VMEM((TB + 8, conv), f32),
        pltpu.VMEM((n, di), f32),
        pltpu.VMEM((1, 128), f32),
        pltpu.VMEM((2 * TB + 8 * nb, di), f32),
    ]
    (nrm, xbc, xc, slope, xd, dts, cc, ct, st, dbf, end, tot, nrme, xbce) = call(
        front_kernel(nw, di, conv, heads), (nt,), ins, outs, scratch, 15,
        [ids, u, ue, gain_in] + wx_parts + [cw, cb, dtb, nr2, tok, e2], "front")
    incoming = carried(tot, end, 1)

    crow = pl.BlockSpec((32, CH), lambda i, s: (0, i))
    srow = pl.BlockSpec((1, CH), lambda i, s: (0, i))
    bspec, cspec = rows(CH, n, di // n), rows(CH, n, di // n + 1)
    (yin,) = call(
        inner_kernel(heads, di), (nc,),
        [bspec, cspec, rows(CH, di), rows(CH, 128), crow, rows(CH, 16), srow],
        [(rows(CH, di), (t, di), bf16)], [], 10,
        [ids, xc, xc, xd, cc, ct, tok, segr], "inner")

    blk = pl.BlockSpec((nb, n, di), lambda i, s: (i, 0, 0))
    outs = [
        (rows(TB, d), (t, d), bf16),
        (rows(TB, di), (t, di), bf16),
        (rows(TB, di), (t, di), bf16),
        (rows(TB, di), (t, di), bf16),
        (rows(TB, di), (t, di), bf16),
        (rows(TB, d), (t, d), bf16),
        (blk, (nc, n, di), bf16),
        (blk, (nc, n, di), f32),
        (rows(TB, 128), (t, 128), f32),
        (whole((8, di)), (8, di), f32),
        (whole((8, di)), (8, di), f32),
        (whole((n, di)), (n, di), f32),
    ]
    ins = [rows(TB, d), rows(TB, di), rows(TB, di), rows(TB, n, di // n + 1), rows(TB, 128), rows(TB, 16), blk,
           pl.BlockSpec((nb, 8, 128), lambda i, s: (i, 0, 0)), whole((n, di)), rows(TB, d), rows(TB, d)]
    ins += [whole(v.shape) for v in wz_parts + wo_parts]
    ins += [whole((1, di)), whole((1, di)), whole((256, di))]
    scratch = [pltpu.VMEM((d, di), bf16), pltpu.VMEM((di, d), bf16)]
    scratch += [pltpu.VMEM((TB, di), f32)] * 3 + [pltpu.VMEM((TB + 8 * nb, di), f32), pltpu.VMEM((TB, di), bf16)]
    (mixed, gn, dz, dy, edy, e, sf, dcs, rin, g_gate, g_skip, reach) = call(
        gate_kernel(nw, di, d), (nt,), ins, outs, scratch, 25,
        [ids, nrm, yin, xc, xc, cc, tok, st, dbf, incoming, u, cot] + wz_parts + wo_parts + [gain_gate, dsk, e2], "gate")
    gend = carried(tot, reach, -1)

    tn = (((0,), (0,)), ((), ()))
    gw_out = lax.dot_general(gn, e, tn, preferred_element_type=f32).astype(bf16)
    gw_z = lax.dot_general(nrm, dz, tn, preferred_element_type=f32).astype(bf16)

    outs = [
        (rows(CH, di), (t, di), bf16),
        (rows(CH, n), (t, n), f32),
        (rows(CH, n), (t, n), f32),
        (rows(CH, 128), (t, 128), f32),
    ]
    (gxd, dbi, dci, rk) = call(
        inner_back_kernel(heads, di), (nc,),
        [bspec, cspec, rows(CH, di), rows(CH, di), rows(CH, 128), crow, rows(CH, 16), srow],
        outs, [pltpu.VMEM((CH, CH), f32), pltpu.VMEM((128, CH), f32)], 20,
        [ids, xc, xc, xd, dy, cc, ct, tok, segr], "inner_back")

    def rev(block, width, col=0):
        return pl.BlockSpec((block, width), lambda i, s: (nt - 1 - i, col))

    rblk = pl.BlockSpec((nb, n, di), lambda i, s: (nt - 1 - i, 0, 0))
    ins = [rev(TB, di), rev(TB, n, di // n), rev(TB, conv), rev(TB, conv), whole((16, conv)), rev(TB, di),
           rev(TB, 256), rev(TB, 128), rev(TB, 16), whole((8, 16)), rev(TB, di), rev(TB, n), rev(TB, n),
           rev(TB, 128), rev(TB, 128), rev(TB, di), rev(TB, di), rblk, rblk, whole((n, di)),
           whole((taps, conv)), whole((1, di)), whole((1, 128)), whole((256, di))]
    outs = [
        (rev(TB, wide), (t, wide), bf16),
        (whole((16, conv)), (16, conv), bf16),
        (whole((8 * taps, conv)), (8 * taps, conv), f32),
        (whole((8, conv)), (8, conv), f32),
        (whole((8, 128)), (8, 128), f32),
        (whole((8, 128)), (8, 128), f32),
    ]
    scratch = [
        pltpu.VMEM((n, di), f32),
        pltpu.VMEM((2 * TB + 8 * nb, di), f32),
        pltpu.VMEM((TB, di), f32),
        pltpu.VMEM((TB + 8, conv), f32),
        pltpu.VMEM((8, 128), bf16),
        pltpu.VMEM((TB, di), bf16),
        pltpu.VMEM((TB, di), bf16),
    ]
    (gpx, edge, g_cw, g_cb, g_a, g_dt) = call(
        back_kernel(di, conv, heads), (nt,), ins, outs, scratch, 25,
        [ids, xc, xc, slope, xbc, xbce, xd, dts, cc, tok, elink, gxd, dbi, dci, rk, rin, dy, edy, sf, dcs, gend,
         cw, dsk, nr, e2], "back")

    gw_x = lax.dot_general(nrm, gpx, tn, preferred_element_type=f32)
    gw_e = lax.dot_general(nrme, edge, tn, preferred_element_type=f32)
    gw_x = jnp.concatenate([gw_x[:, :conv] + gw_e, gw_x[:, conv : conv + heads]], axis=1).astype(bf16)
    edge_in = shift(edge, "seq", -1)

    ins = [rows(TB, di), rows(TB, wide), whole((16, conv)), rows(TB, d), rows(TB, d)]
    ins += [whole(v.shape) for v in wz_parts + wx_parts] + [whole((1, d))]
    outs = [(rows(TB, d), (t, d), bf16), (whole((8, d)), (8, d), f32)]
    (grad_input, g_gain) = call(
        input_kernel(nw, di, conv, heads), (nt,), ins, outs,
        [pltpu.VMEM((d, di), bf16), pltpu.VMEM((d, wide), bf16)], 12,
        [ids, dz, gpx, edge_in, u, e] + wz_parts + wx_parts + [gain_in], "input")

    r_out, r_z, r_x = reduce_rows(gw_out), reduce_rows(gw_z), reduce_rows(gw_x)
    parts = [
        g_cw.reshape(taps, 8, conv).sum(1).reshape(-1),
        g_cb.sum(0),
        g_a.sum(0)[:heads] * rate[0],
        g_skip.sum(0).reshape(heads, p).sum(1),
        g_dt.sum(0)[:heads],
        g_gain.sum(0),
        g_gate.sum(0),
    ]
    total = lax.psum(jnp.concatenate(parts), ("seq", "wshard"))
    w = lax.axis_index("wshard")
    res, off = [], 0
    for k, part in enumerate(parts):
        v = total[off : off + part.shape[0]]
        off += part.shape[0]
        v = v.reshape(taps, conv) if k == 0 else v
        width = v.shape[-1] // nw
        res.append(lax.dynamic_slice_in_dim(v, w * width, width, axis=v.ndim - 1))
    return (mixed[None], grad_input[None], jnp.concatenate([r_z, r_x], axis=1), r_out) + tuple(res)


def solution(mesh):
    wide = P("wshard", "seq", None)
    mat = P("wshard", None)
    taps = P(None, "wshard")
    vec = P("wshard")
    return jax.shard_map(
        body,
        mesh=mesh,
        in_specs=(wide, wide, mat, mat, mat, taps) + (vec,) * 6,
        out_specs=(wide, wide, mat, mat, taps) + (vec,) * 6,
        check_vma=False,
    )
```

time: 1210 us -> 424 us (0.35)
  matrix products: 302 us -> 14.7 us
  waiting for transfers between devices: 353 us -> 71.8 us
  local copies, waits for them, and re-layouts: 222 us -> 38 us
  other arithmetic: 189 us -> 30.4 us
  Pallas kernels: 0 us -> 138 us
  starting transfers between devices: 5.23 us -> 67.3 us
  blocking collectives: 92.9 us -> 57.7 us
  between operations: 20.7 us -> 2.49 us
  loops' own time: 12.1 us -> 0 us
    dot_general x60 -> x4, matrix products: 302 us -> 14.7 us  [the longest x1 5.64 us: body(): gw_x = lax.dot_general(nrm, gpx, tn, preferred_element_type=f32)]
    all_gather x4 -> x0, waiting for transfers between devices: 159 us -> none  [the longest x2 139 us: carried_in(): everything = jax.tree.map(lambda part: lax.all_gather(part, axis), shard)]
    pallas_call x0 -> x6, Pallas kernels: none -> 138 us  [call(): pl.pallas_call(kernel, grid_spec=pltpu.PrefetchScalarGridSpec(num_scalar_...]
    psum x1 -> x0, waiting for transfers between devices: 102 us -> none  [body(): lax.psum((shards[0], shards[1], shards[2], shards[3], shards[4], shards[5...]
    reduce_scatter x2 -> x0, waiting for transfers between devices: 84.9 us -> none  [the longest x1 84.9 us: body(): lax.psum_scatter(grad_w_in, 'wshard', scatter_dimension=0, tiled=True)]
    ppermute x2 -> x41, waiting for transfers between devices: 5.62 us -> 71.8 us  [the longest x33 64.4 us: swap(): lax.ppermute(v, axis, [(k, k ^ bit) for k in range(lax.axis_size(axis))])]
    ppermute x2 -> x41, starting transfers between devices: 4.7 us -> 67.3 us  [the longest x8 34.1 us: shift(): lax.ppermute(v, axis, [(k, k + steps) for k in range(n) if 0 <= k + steps...]
    reduce_sum x16 -> x9, other arithmetic: 57.1 us -> 5.68 us  [the longest x1 1.34 us: body(): g_gain.sum(0)]
  transfers between devices with their start and end apart: 10 -> 41, of which waited for: 6 -> 14; matrix products, arithmetic and copies ran while one was open for 43% -> 17% of each run, Pallas kernels for 0% -> 19%
where the time goes in v1:
time: 424 us; the launch traced here: 421 us
  Pallas kernels  138 us (33%)
  waiting for transfers between devices  71.8 us (17%)
  starting transfers between devices  67.3 us (16%)
  blocking collectives  57.7 us (14%)
  local copies, waits for them, and re-layouts  38 us (9%)
  other arithmetic  30.4 us (7%)
  matrix products  14.7 us (3%)
    pallas_call x6, Pallas kernels, call(): pl.pallas_call(kernel, grid_spec=pltpu.PrefetchScalarGridSpec(num_scalar_...  138 us
    ppermute x33, waiting for transfers between devices, swap(): lax.ppermute(v, axis, [(k, k ^ bit) for k in range(lax.axis_size(axis))])  64.4 us
    psum x1, blocking collectives, body(): total = lax.psum(jnp.concatenate(parts), ('seq', 'wshard'))  45.6 us
    ppermute x8, starting transfers between devices, shift(): lax.ppermute(v, axis, [(k, k + steps) for k in range(n) if 0 <= k + steps...  34.1 us
    ppermute x33, starting transfers between devices, swap(): lax.ppermute(v, axis, [(k, k ^ bit) for k in range(lax.axis_size(axis))])  33.2 us
    unnamed x1, blocking collectives  12 us
  transfers between devices with their start and end apart: 41, of which 14 were waited for; matrix products, arithmetic and copies ran while one was open for 17% of the time, Pallas kernels for 19%

profile of v1, /device:TPU:0, one launch (start us, length us, event | category | flops | bytes accessed | tf_op | source)
XLA Modules:
  0.0 420.6 jit_solution(8413012144699213946)
XLA Ops:
  12.9 4.1 concatenate.80
  17.3 12.0 %all-reduce.7 = bf16[11336]{0:T(1024)(128)(2,1)S(1)} all-reduce(bf16[11336]{0:T(1024)(128)(2,1)S(1)} %dynamic-update-slice), channel_id=2, replica_groups=mesh['seq'=8,'wshard'=4] {'wshard'}, use_global_device_ids=true, to_apply=%add.7 | all-reduce | flops 11336 | bytes 45344
  37.4 20.5 %front.1 = (bf16[1024,768]{1,0:T(8,128)(2,1)}, bf16[1024,1792]{1,0:T(8,128)(2,1)}, bf16[1024,1792]{1,0:T(8,128)(2,1)}, bf16[1024,1792]{1,0:T(8,128)(2,1)}, bf16[...) custom-call(s32[4]{0:T(128)} %pad_add_fusion.ids, ...), custom_call_target="tpu_custom_call" | custom-call | flops 16499999744 | bytes 1048576 | tf_op jit(solution)/shard_map/front/pallas_call | solution.py:45
  67.0 6.6 %collective-permute-done.4 = bf16[144,1536]{1,0:T(8,128)(2,1)S(1)} collective-permute-done((bf16[144,1536]{1,0:T(8,128)(2,1)S(1)}, bf16[144,1536]{1,0:T(8,128)(2,1)S(1)}, u32[]{:S(2)}, u32[]{:S(2)}) %collective-permute-start.4) | collective-permute-done | bytes 442400 | tf_op jit(solution)/shard_map/ppermute | solution.py:466
  73.8 6.1 %collective-permute-start.5 = (bf16[144,1536]{1,0:T(8,128)(2,1)S(1)}, bf16[144,1536]{1,0:T(8,128)(2,1)}, u32[]{:S(2)}, u32[]{:S(2)}) collective-permute-start(bf16[144,1536]{1,0:T(8,128)(2,1)S(1)} %pad_maximum_fusion.4), channel_id=1, source_target_pairs={{0,8},{4,12},{8,16},{12,20},{16,24},{20,28},{1,9},{5,13},{9,17},{1... | collective-permute-start | bytes 1327112 | tf_op jit(solution)/shard_map/ppermute | solution.py:466
  82.7 10.5 %collective-permute-done.10.rest_5_ = bf16[384,768]{1,0:T(8,128)(2,1)} collective-permute-done((bf16[384,768]{1,0:T(8,128)(2,1)}, bf16[384,768]{1,0:T(8,128)(2,1)}, u32[]{:S(2)}, u32[]{:S(2)}) %collective-permute-start.10) | collective-permute-done | bytes 589856 | tf_op jit(solution)/shard_map/ppermute | solution.py:461
  94.5 3.7 collective-permute-start.6
  98.1 10.1 %inner.1.yin = bf16[1024,1536]{1,0:T(8,128)(2,1)} custom-call(s32[4]{0:T(128)} %pad_add_fusion.ids, bf16[1024,1792]{1,0:T(8,128)(2,1)} %get-tuple-element.50.b.c.x.c_in.xc.b_in, bf16[1024,1792]{1,0:T(8,128)(2,1)} %get-tuple-element.50.b.c.x.c_in.xc.b_in, bf16[1024,1536]{1,0:T(8,128)(2,1)} %get-tuple-element.51.xd, f32[1024,128]{1,0:T(8,128)} %get-tuple-element.52.cc, ...), custom_call_target="tpu_custom_call" | custom-call | flops 11000000512 | bytes 1048576 | tf_op jit(solution)/shard_map/inner/pallas_call | solution.py:45
  109.0 37.5 %gate.1 = (bf16[1024,768]{1,0:T(8,128)(2,1)}, bf16[1024,1536]{1,0:T(8,128)(2,1)}, bf16[1024,1536]{1,0:T(8,128)(2,1)}, bf16[1024,1536]{1,0:T(8,128)(2,1)}, bf16[1...) custom-call(s32[4]{0:T(128)} %pad_add_fusion.ids, ...), custom_call_target="tpu_custom_call" | custom-call | flops 27499999232 | bytes 1048576 | tf_op jit(solution)/shard_map/gate/pallas_call | solution.py:45
  149.0 5.2 %convolution_convert_fusion = bf16[1536,768]{1,0:T(8,128)(2,1)S(1)} fusion(bf16[1024,1536]{1,0:T(8,128)(2,1)} %get-tuple-element.79, bf16[1024,768]{1,0:T(8,128)(2,1)} %get-tuple-element.76.e), kind=kOutput, calls=%fused_computation.4 | convolution fusion | flops 2417098752 | bytes 7077888 | tf_op jit(solution)/shard_map/dot_general | solution.py:665
  164.2 24.6 %inner_back.1 = (bf16[1024,1536]{1,0:T(8,128)(2,1)}, f32[1024,128]{1,0:T(8,128)}, f32[1024,128]{1,0:T(8,128)}, f32[1024,128]{1,0:T(8,128)}) custom-call(s32[4]{0:T(128)} %pad_add_fusion.ids, bf16[1024,1792]{1,0:T(8,128)(2,1)} %get-tuple-element.50.b.c.x.c_in.xc.b_in, bf16[1024,1792]{1,0:T(8,128)(2,1)} %get-tuple-element.50.b.c.x.c_in.xc.b_in, ...), custom_call_target="tpu_custom_call" | custom-call | flops 22000001024 | bytes 1048576 | tf_op jit(solution)/shard_map/inner_back/pallas_call | solution.py:45
  190.9 13.6 %collective-permute-start.15 = (bf16[128,1536]{1,0:T(8,128)(2,1)S(1)}, bf16[128,1536]{1,0:T(8,128)(2,1)S(1)}, u32[]{:S(2)}, u32[]{:S(2)}) collective-permute-start(bf16[128,1536]{1,0:T(8,128)(2,1)S(1)} %add_convert_fusion.4), channel_id=1, source_target_pairs={{4,0},{8,4},{12,8},{16,12},{20,16},{24,20},{28,24},{5,1},{9,5},{13... | collective-permute-start | bytes 1179656 | tf_op jit(solution)/shard_map/ppermute | solution.py:466
  212.1 30.4 %back.1 = (bf16[1024,1920]{1,0:T(8,128)(2,1)}, bf16[16,1792]{1,0:T(8,128)(2,1)}, f32[32,1792]{1,0:T(8,128)}, f32[8,1792]{1,0:T(8,128)}, f32[8,128]{1,0:T(8,128)}, /*index=5*/f32[8,128]{1,0:T(8,128)}) custom-call(s32[4]{0:T(128)} %pad_add_fusion.ids, bf16[1024,1792]{1,0:T(8,128)(2,1)} %get-tuple-element.50.b.c.x.c_in.xc.b_in, ...), custom_call_target="tpu_custom_call" | custom-call | flops 27499999232 | bytes 1048576 | tf_op jit(solution)/shard_map/back/pallas_call | solution.py:45
  246.6 5.6 %fusion.33 = f32[768,1920]{1,0:T(8,128)S(1)} fusion(bf16[1024,768]{1,0:T(8,128)(2,1)S(1)} %copy-done.21, bf16[1024,1920]{1,0:T(8,128)(2,1)} %get-tuple-element.74.gpx), kind=kOutput, calls=%fused_computation.151 | convolution fusion | flops 3019898880 | bytes 11403264 | tf_op jit(solution)/shard_map/dot_general | solution.py:710
  256.4 15.3 %input.1 = (bf16[1024,768]{1,0:T(8,128)(2,1)}, f32[8,768]{1,0:T(8,128)}) custom-call(s32[4]{0:T(128)} %pad_add_fusion.ids, bf16[1024,1536]{1,0:T(8,128)(2,1)} %get-tuple-element.59.gpz, bf16[1024,1920]{1,0:T(8,128)(2,1)} %get-tuple-element.74.gpx, bf16[16,1792]{1,0:T(8,128)(2,1)} %collective-permute-done.16.edge, bf16[1024,768]{1,0:T(8,128)(2,1)} %bitcast.147, ...), custom_call_target="tpu_custom_call" | custom-call | flops 13200000000 | bytes 1048576 | tf_op jit(solution)/shard_map/input/pallas_call | solution.py:45
  274.4 45.6 %psum.7 = f32[11336]{0:T(1024)} all-reduce(f32[11336]{0:T(1024)} %concatenate.106), channel_id=1, replica_groups=mesh['seq'=8,'wshard'=4] {'seq','wshard'}, use_global_device_ids=true, to_apply=%region_10.11 | all-reduce | flops 11336 | bytes 90688 | tf_op jit(solution)/shard_map/psum | solution.py:733
  337.5 6.6 %collective-permute-done.35 = bf16[192,768]{1,0:T(8,128)(2,1)S(1)} collective-permute-done((bf16[192,768]{1,0:T(8,128)(2,1)S(1)}, bf16[192,768]{1,0:T(8,128)(2,1)S(1)}, u32[]{:S(2)}, u32[]{:S(2)}) %collective-permute-start.35) | collective-permute-done | bytes 294944 | tf_op jit(solution)/shard_map/ppermute | solution.py:461
  365.9 9.1 %collective-permute-done.26 = bf16[1,192,1816]{2,1,0:T(8,128)(2,1)S(1)} collective-permute-done((bf16[1,192,1816]{2,1,0:T(8,128)(2,1)S(1)}, bf16[1,192,1816]{2,1,0:T(8,128)(2,1)S(1)}, u32[]{:S(2)}, u32[]{:S(2)}) %collective-permute-start.26) | collective-permute-done | bytes 697376 | tf_op jit(solution)/shard_map/ppermute | solution.py:461
  378.8 7.2 %collective-permute-done.27 = bf16[96,1816]{1,0:T(8,128)(2,1)S(1)} collective-permute-done((bf16[96,1816]{1,0:T(8,128)(2,1)S(1)}, bf16[96,1816]{1,0:T(8,128)(2,1)S(1)}, u32[]{:S(2)}, u32[]{:S(2)}) %collective-permute-start.27) | collective-permute-done | bytes 348704 | tf_op jit(solution)/shard_map/ppermute | solution.py:461
  389.0 3.7 collective-permute-done.28
  393.8 5.5 %collective-permute-done.29 = bf16[24,1816]{1,0:T(8,128)(2,1)S(1)} collective-permute-done((bf16[24,1816]{1,0:T(8,128)(2,1)S(1)}, bf16[24,1816]{1,0:T(8,128)(2,1)S(1)}, u32[]{:S(2)}, u32[]{:S(2)}) %collective-permute-start.29) | collective-permute-done | bytes 87200 | tf_op jit(solution)/shard_map/ppermute | solution.py:461
  401.0 4.2 %collective-permute-done.30 = bf16[24,1816]{1,0:T(8,128)(2,1)S(1)} collective-permute-done((bf16[24,1816]{1,0:T(8,128)(2,1)S(1)}, bf16[24,1816]{1,0:T(8,128)(2,1)S(1)}, u32[]{:S(2)}, u32[]{:S(2)}) %collective-permute-start.30) | collective-permute-done | bytes 87200 | tf_op jit(solution)/shard_map/ppermute | solution.py:461
  406.6 4.3 %collective-permute-done.31 = bf16[48,1816]{1,0:T(8,128)(2,1)S(1)} collective-permute-done((bf16[48,1816]{1,0:T(8,128)(2,1)S(1)}, bf16[48,1816]{1,0:T(8,128)(2,1)S(1)}, u32[]{:S(2)}, u32[]{:S(2)}) %collective-permute-start.31) | collective-permute-done | bytes 174368 | tf_op jit(solution)/shard_map/ppermute | solution.py:461
  412.0 6.6 %collective-permute-done.32 = bf16[96,1816]{1,0:T(8,128)(2,1)S(1)} collective-permute-done((bf16[96,1816]{1,0:T(8,128)(2,1)S(1)}, bf16[96,1816]{1,0:T(8,128)(2,1)S(1)}, u32[]{:S(2)}, u32[]{:S(2)}) %collective-permute-start.32) | collective-permute-done | bytes 348704 | tf_op jit(solution)/shard_map/ppermute | solution.py:461
  (268 shorter events, 119.5 us)
Async XLA Ops:
  1.8 34.7 %collective-permute-start.2 = (bf16[192,1816]{1,0:T(8,128)(2,1)S(1)}, bf16[192,1816]{1,0:T(8,128)(2,1)S(1)}, u32[]{:S(2)}, u32[]{:S(2)}) collective-permute-start(bf16[192,1816]{1,0:T(8,128)(2,1)S(1)} %slice.160.rest_0_.rest_4_), channel_id=1, source_target_pairs={{0,1},{1,0},{2,3},{3,2},{4,5},{5,4},{6,7},{7,6},{8,9},{9,8},{10,11... | collective-permute-start | bytes 2092040 | tf_op jit(solution)/shard_map/ppermute | solution.py:461
  2.3 27.7 %collective-permute-start.1 = (bf16[192,1816]{1,0:T(8,128)(2,1)S(1)}, bf16[192,1816]{1,0:T(8,128)(2,1)}, u32[]{:S(2)}, u32[]{:S(2)}) collective-permute-start(bf16[192,1816]{1,0:T(8,128)(2,1)S(1)} %slice.160.rest_0_.rest_4_), channel_id=1, source_target_pairs={{0,2},{1,3},{2,0},{3,1},{4,6},{5,7},{6,4},{7,5},{8,10},{9,11},{10,... | collective-permute-start | bytes 2092040 | tf_op jit(solution)/shard_map/ppermute | solution.py:461
  5.7 30.9 %collective-permute-start = (bf16[16,768]{1,0:T(8,128)(2,1)S(1)}, bf16[16,768]{1,0:T(8,128)(2,1)S(1)}, u32[]{:S(2)}, u32[]{:S(2)}) collective-permute-start(bf16[16,768]{1,0:T(8,128)(2,1)S(1)} %slice_bitcast_fusion), channel_id=1, source_target_pairs={{0,4},{4,8},{8,12},{12,16},{16,20},{20,24},{24,28},{1,5},{5,9},{9,... | collective-permute-start | bytes 73736 | tf_op jit(solution)/shard_map/ppermute | solution.py:466
  64.7 43.5 %collective-permute-start.8 = (bf16[192,1536]{1,0:T(8,128)(2,1)S(1)}, bf16[192,1536]{1,0:T(8,128)(2,1)}, u32[]{:S(2)}, u32[]{:S(2)}) collective-permute-start(bf16[192,1536]{1,0:T(8,128)(2,1)S(1)} %slice.184.rest_0_), channel_id=1, source_target_pairs={{0,1},{1,0},{2,3},{3,2},{4,5},{5,4},{6,7},{7,6},{8,9},{9,8},{10,11... | collective-permute-start | bytes 1769480 | tf_op jit(solution)/shard_map/ppermute | solution.py:461
  65.0 17.8 %collective-permute-start.7 = (bf16[192,1536]{1,0:T(8,128)(2,1)S(1)}, bf16[192,1536]{1,0:T(8,128)(2,1)}, u32[]{:S(2)}, u32[]{:S(2)}) collective-permute-start(bf16[192,1536]{1,0:T(8,128)(2,1)S(1)} %slice.184.rest_0_), channel_id=1, source_target_pairs={{0,2},{1,3},{2,0},{3,1},{4,6},{5,7},{6,4},{7,5},{8,10},{9,11},{10,... | collective-permute-start | bytes 1769480 | tf_op jit(solution)/shard_map/ppermute | solution.py:461
  65.5 27.8 %collective-permute-start.10 = (bf16[384,768]{1,0:T(8,128)(2,1)}, bf16[384,768]{1,0:T(8,128)(2,1)}, u32[]{:S(2)}, u32[]{:S(2)}) collective-permute-start(bf16[384,768]{1,0:T(8,128)(2,1)} %rest_4_.1), channel_id=1, source_target_pairs={{0,2},{1,3},{2,0},{3,1},{4,6},{5,7},{6,4},{7,5},{8,10},{9,11},{10,... | collective-permute-start | bytes 1769480 | tf_op jit(solution)/shard_map/ppermute | solution.py:461
  67.0 41.2 %collective-permute-start.11 = (bf16[384,768]{1,0:T(8,128)(2,1)}, bf16[384,768]{1,0:T(8,128)(2,1)}, u32[]{:S(2)}, u32[]{:S(2)}) collective-permute-start(bf16[384,768]{1,0:T(8,128)(2,1)} %rest_4_.1), channel_id=1, source_target_pairs={{0,1},{1,0},{2,3},{3,2},{4,5},{5,4},{6,7},{7,6},{8,9},{9,8},{10,11... | collective-permute-start | bytes 1769480 | tf_op jit(solution)/shard_map/ppermute | solution.py:461
  73.8 19.5 %collective-permute-start.5 = (bf16[144,1536]{1,0:T(8,128)(2,1)S(1)}, bf16[144,1536]{1,0:T(8,128)(2,1)}, u32[]{:S(2)}, u32[]{:S(2)}) collective-permute-start(bf16[144,1536]{1,0:T(8,128)(2,1)S(1)} %pad_maximum_fusion.4), channel_id=1, source_target_pairs={{0,8},{4,12},{8,16},{12,20},{16,24},{20,28},{1,9},{5,13},{9,17},{1... | collective-permute-start | bytes 1327112 | tf_op jit(solution)/shard_map/ppermute | solution.py:466
  82.7 25.5 %collective-permute-start.9 = (bf16[192,1536]{1,0:T(8,128)(2,1)}, bf16[192,1536]{1,0:T(8,128)(2,1)}, u32[]{:S(2)}, u32[]{:S(2)}) collective-permute-start(bf16[192,1536]{1,0:T(8,128)(2,1)} %collective-permute-done.7.rest_1_), channel_id=1, source_target_pairs={{0,1},{1,0},{2,3},{3,2},{4,5},{5,4},{6,7},{7,6},{8,9},{9,8},{10,11... | collective-permute-start | bytes 1769480 | tf_op jit(solution)/shard_map/ppermute | solution.py:461
  93.3 15.0 %collective-permute-start.12 = (bf16[384,768]{1,0:T(8,128)(2,1)}, bf16[384,768]{1,0:T(8,128)(2,1)}, u32[]{:S(2)}, u32[]{:S(2)}) collective-permute-start(bf16[384,768]{1,0:T(8,128)(2,1)} %collective-permute-done.10.rest_5_), channel_id=1, source_target_pairs={{0,1},{1,0},{2,3},{3,2},{4,5},{5,4},{6,7},{7,6},{8,9},{9,8},{10,11... | collective-permute-start | bytes 1769480 | tf_op jit(solution)/shard_map/ppermute | solution.py:461
  94.5 13.8 %collective-permute-start.6 = (bf16[128,1536]{1,0:T(8,128)(2,1)S(1)}, bf16[128,1536]{1,0:T(8,128)(2,1)S(1)}, u32[]{:S(2)}, u32[]{:S(2)}) collective-permute-start(bf16[128,1536]{1,0:T(8,128)(2,1)S(1)} %add_convert_fusion.5), channel_id=1, source_target_pairs={{0,4},{4,8},{8,12},{12,16},{16,20},{20,24},{24,28},{1,5},{5,9},{9,... | collective-permute-start | bytes 1179656 | tf_op jit(solution)/shard_map/ppermute | solution.py:466
  147.7 14.2 %collective-permute-start.13 = (bf16[144,1536]{1,0:T(8,128)(2,1)S(1)}, bf16[144,1536]{1,0:T(8,128)(2,1)S(1)}, u32[]{:S(2)}, u32[]{:S(2)}) collective-permute-start(bf16[144,1536]{1,0:T(8,128)(2,1)S(1)} %pad_maximum_fusion), channel_id=1, source_target_pairs={{4,0},{8,4},{12,8},{16,12},{20,16},{24,20},{28,24},{5,1},{9,5},{13... | collective-permute-start | bytes 1327112 | tf_op jit(solution)/shard_map/ppermute | solution.py:466
  155.3 49.2 %collective-permute-start.33 = (bf16[2,384,768]{2,1,0:T(8,128)(2,1)}, bf16[2,384,768]{2,1,0:T(8,128)(2,1)}, u32[]{:S(2)}, u32[]{:S(2)}) collective-permute-start(bf16[2,384,768]{2,1,0:T(8,128)(2,1)} %dynamic-slice_bitcast_fusion), channel_id=1, source_target_pairs={{0,1},{1,0},{2,3},{3,2},{4,5},{5,4},{6,7},{7,6},{8,9},{9,8},{10,11... | collective-permute-start | bytes 3538952 | tf_op jit(solution)/shard_map/ppermute | solution.py:461
  160.8 46.4 %collective-permute-start.17 = (bf16[2,192,1536]{2,1,0:T(8,128)(2,1)}, bf16[2,192,1536]{2,1,0:T(8,128)(2,1)}, u32[]{:S(2)}, u32[]{:S(2)}) collective-permute-start(bf16[2,192,1536]{2,1,0:T(8,128)(2,1)} %dynamic-slice_bitcast_fusion.1), channel_id=1, source_target_pairs={{0,1},{1,0},{2,3},{3,2},{4,5},{5,4},{6,7},{7,6},{8,9},{9,8},{10,11... | collective-permute-start | bytes 3538952 | tf_op jit(solution)/shard_map/ppermute | solution.py:461
  162.9 26.7 %collective-permute-start.14 = (bf16[144,1536]{1,0:T(8,128)(2,1)}, bf16[144,1536]{1,0:T(8,128)(2,1)}, u32[]{:S(2)}, u32[]{:S(2)}) collective-permute-start(bf16[144,1536]{1,0:T(8,128)(2,1)} %pad_maximum_fusion.5), channel_id=1, source_target_pairs={{8,0},{12,4},{16,8},{20,12},{24,16},{28,20},{9,1},{13,5},{17,9},{2... | collective-permute-start | bytes 1327112 | tf_op jit(solution)/shard_map/ppermute | solution.py:466
  190.9 20.4 %collective-permute-start.15 = (bf16[128,1536]{1,0:T(8,128)(2,1)S(1)}, bf16[128,1536]{1,0:T(8,128)(2,1)S(1)}, u32[]{:S(2)}, u32[]{:S(2)}) collective-permute-start(bf16[128,1536]{1,0:T(8,128)(2,1)S(1)} %add_convert_fusion.4), channel_id=1, source_target_pairs={{4,0},{8,4},{12,8},{16,12},{20,16},{24,20},{28,24},{5,1},{9,5},{13... | collective-permute-start | bytes 1179656 | tf_op jit(solution)/shard_map/ppermute | solution.py:466
  206.5 125.9 %collective-permute-start.34 = (bf16[1,384,768]{2,1,0:T(8,128)(2,1)S(1)}, bf16[1,384,768]{2,1,0:T(8,128)(2,1)}, u32[]{:S(2)}, u32[]{:S(2)}) collective-permute-start(bf16[1,384,768]{2,1,0:T(8,128)(2,1)S(1)} %constant_dynamic-slice_fusion.1), channel_id=1, source_target_pairs={{0,2},{1,3},{2,0},{3,1},{4,6},{5,7},{6,4},{7,5},{8,10},{9,11},{10,... | collective-permute-start | bytes 1769480 | tf_op jit(solution)/shard_map/ppermute | solution.py:461
  210.0 126.1 %collective-permute-start.18 = (bf16[1,192,1536]{2,1,0:T(8,128)(2,1)}, bf16[1,192,1536]{2,1,0:T(8,128)(2,1)}, u32[]{:S(2)}, u32[]{:S(2)}) collective-permute-start(bf16[1,192,1536]{2,1,0:T(8,128)(2,1)} %constant_dynamic-slice_fusion.3), channel_id=1, source_target_pairs={{0,2},{1,3},{2,0},{3,1},{4,6},{5,7},{6,4},{7,5},{8,10},{9,11},{10,... | collective-permute-start | bytes 1769480 | tf_op jit(solution)/shard_map/ppermute | solution.py:461
  254.5 104.7 %collective-permute-start.25 = (bf16[2,192,1816]{2,1,0:T(8,128)(2,1)}, bf16[2,192,1816]{2,1,0:T(8,128)(2,1)}, u32[]{:S(2)}, u32[]{:S(2)}) collective-permute-start(bf16[2,192,1816]{2,1,0:T(8,128)(2,1)} %fusion.5), channel_id=1, source_target_pairs={{0,1},{1,0},{2,3},{3,2},{4,5},{5,4},{6,7},{7,6},{8,9},{9,8},{10,11... | collective-permute-start | bytes 4184072 | tf_op jit(solution)/shard_map/ppermute | solution.py:461
  361.0 14.0 %collective-permute-start.26 = (bf16[1,192,1816]{2,1,0:T(8,128)(2,1)S(1)}, bf16[1,192,1816]{2,1,0:T(8,128)(2,1)S(1)}, u32[]{:S(2)}, u32[]{:S(2)}) collective-permute-start(bf16[1,192,1816]{2,1,0:T(8,128)(2,1)S(1)} %constant_dynamic-slice_fusion.2), channel_id=1, source_target_pairs={{0,2},{1,3},{2,0},{3,1},{4,6},{5,7},{6,4},{7,5},{8,10},{9,11},{10,... | collective-permute-start | bytes 2092040 | tf_op jit(solution)/shard_map/ppermute | solution.py:461
  362.9 14.2 %collective-permute-start.22 = (bf16[24,1536]{1,0:T(8,128)(2,1)S(1)}, bf16[24,1536]{1,0:T(8,128)(2,1)S(1)}, u32[]{:S(2)}, u32[]{:S(2)}) collective-permute-start(bf16[24,1536]{1,0:T(8,128)(2,1)S(1)} %fusion.18), channel_id=1, source_target_pairs={{0,16},{4,20},{8,24},{12,28},{16,0},{20,4},{24,8},{28,12},{1,17},{... | collective-permute-start | bytes 221192 | tf_op jit(solution)/shard_map/ppermute | solution.py:461
  365.9 22.2 %collective-permute-start.39 = (bf16[96,768]{1,0:T(8,128)(2,1)S(1)}, bf16[96,768]{1,0:T(8,128)(2,1)S(1)}, u32[]{:S(2)}, u32[]{:S(2)}) collective-permute-start(bf16[96,768]{1,0:T(8,128)(2,1)S(1)} %pad_maximum_fusion.11), channel_id=1, source_target_pairs={{0,8},{4,12},{8,0},{12,4},{16,24},{20,28},{24,16},{28,20},{1,9},{5... | collective-permute-start | bytes 442376 | tf_op jit(solution)/shard_map/ppermute | solution.py:461
  377.1 16.6 %collective-permute-start.23 = (bf16[48,1536]{1,0:T(8,128)(2,1)S(1)}, bf16[48,1536]{1,0:T(8,128)(2,1)S(1)}, u32[]{:S(2)}, u32[]{:S(2)}) collective-permute-start(bf16[48,1536]{1,0:T(8,128)(2,1)S(1)} %pad_maximum_fusion.10), channel_id=1, source_target_pairs={{0,8},{4,12},{8,0},{12,4},{16,24},{20,28},{24,16},{28,20},{1,9},{5... | collective-permute-start | bytes 442376 | tf_op jit(solution)/shard_map/ppermute | solution.py:461
  388.1 17.2 %collective-permute-start.40 = (bf16[192,768]{1,0:T(8,128)(2,1)S(1)}, bf16[192,768]{1,0:T(8,128)(2,1)S(1)}, u32[]{:S(2)}, u32[]{:S(2)}) collective-permute-start(bf16[192,768]{1,0:T(8,128)(2,1)S(1)} %pad_maximum_fusion.8), channel_id=1, source_target_pairs={{0,4},{4,0},{8,12},{12,8},{16,20},{20,16},{24,28},{28,24},{1,5},{5... | collective-permute-start | bytes 884744 | tf_op jit(solution)/shard_map/ppermute | solution.py:461
  (40 other events, 363.6 us)

commit v2 on v1

--- a/solution.py
+++ b/solution.py
@@ -38,7 +38,7 @@
 
 
 def cost(us):
-    return pl.CostEstimate(flops=int(us * 1.1e9), bytes_accessed=1 << 20, transcendentals=0)
+    return pl.CostEstimate(flops=int(us * 1.1e8), bytes_accessed=1 << 20, transcendentals=0)
 
 
 def call(kernel, grid, ins, outs, scratch, us, args, name):
@@ -263,11 +263,10 @@
     return kernel
 
 
-def inner_back_kernel(heads, di):
-    p = di // heads
+def inner_back_kernel(p, h0, h1):
     per = 128 // p
 
-    def kernel(ids, b, c, xd, dy, cc, ct, tok, segr, gxd_o, db_o, dc_o, rk_o, gs, rr):
+    def kernel(ids, b, c, xd, dy, cc, ct, tok, segr, gxd_o, db_o, dc_o, rk_o, rr):
         st = dot_nt(b[...], c[...])
         si = lax.broadcasted_iota(jnp.int32, (CH, CH), 0)
         ti = lax.broadcasted_iota(jnp.int32, (CH, CH), 1)
@@ -276,7 +275,7 @@
         rr[...] = jnp.zeros_like(rr)
         rk_o[...] = jnp.zeros_like(rk_o)
         gsum = jnp.zeros((CH, CH), f32)
-        for j in range(heads // per):
+        for j in range((h1 - h0) // per):
             xp = xd[:, 128 * j : 128 * j + 128]
             dyp = dy[:, 128 * j : 128 * j + 128]
             dys = jnp.concatenate(
@@ -285,7 +284,7 @@
             gm = dot_nt(xp, dys)
             ms = []
             for q in range(per):
-                h = per * j + q
+                h = h0 + per * j + q
                 e = jnp.exp2(ct[h : h + 1, :] - cc[:, h : h + 1] + bias)
                 ms.append((st * e).astype(bf16))
                 ge = gm[:, q * CH : (q + 1) * CH] * e
@@ -302,23 +301,34 @@
     return kernel
 
 
-def back_kernel(di, conv, heads):
-    def kernel(ids, xc, b_in, slope, xbc, xbce, xd, dts, cc, tok, elink, gxd, dbi, dci, rk, rin, dy, edy,
-               sf, dcs, gend, cw, dsk, nr, e2, gp_o, edge_o, gw_o, gb_o, ga_o, gdt_o,
-               ds, sp, sr, ext, xw, xq, xe):
+def back_kernel(w, n, h0, h1, last_part):
+    cols = w + 2 * n if last_part else w
+
+    def kernel(ids, x_in, b_in, slope, xbc, xbce, xd, dts, cc, tok, elink, gxd, dbi, dci, rk, rin,
+               dy, edy, sf, dcs, gend, cw, dsk, nr, e2, *rest):
+        if last_part:
+            slope2, xbc2, xbce2, cw2, dbp, dcp, ddtp = rest[:7]
+            gp_o, edge_o, gw_o, gb_o, ga_o, gdt_o = rest[7:13]
+        else:
+            gp_o, edge_o, gw_o, gb_o, ga_o, gdt_o, dbp_o, dcp_o, ddtp_o = rest[:9]
+        ds, sp, sr, ext, xq, xe = rest[-6:]
         i = pl.program_id(0)
-        n = (conv - di) // 2
         nb = TB // CH
+
+        def pick(a, a2, r, c0):
+            return a[r, c0 : c0 + 256] if c0 < w else a2[r, c0 - w : c0 - w + 256]
 
         @pl.when(i == 0)
         def _():
             ds[...] = gend[...].astype(f32)
-            ext[TB : TB + 8, :] = jnp.zeros((8, conv), f32)
+            ext[TB : TB + 8, :] = jnp.zeros((8, cols), f32)
             gw_o[...] = jnp.zeros_like(gw_o)
             gb_o[...] = jnp.zeros_like(gb_o)
             ga_o[...] = jnp.zeros_like(ga_o)
             gdt_o[...] = jnp.zeros_like(gdt_o)
 
+        if not last_part:
+            slope2 = xbc2 = xbce2 = cw2 = None
         dt = dts[:, :128]
         pieces, leaves = [dt], []
         for k in range(nb):
@@ -334,7 +344,7 @@
             lacc = []
             gb = dbi[r, :]
             gc = dci[r, :]
-            for c0 in range(0, di, 256):
+            for c0 in range(0, w, 256):
                 c = slice(c0, c0 + 256)
                 dsv = ds[:, c]
                 dsb = dsv.astype(bf16)
@@ -346,20 +356,24 @@
                 lacc.append(jnp.sum(dsv * sfv.astype(f32), axis=0, keepdims=True))
                 lvr = sp[2 * TB + 8 * k : 2 * TB + 8 * k + 1, c]
                 ds[:, c] = lvr * dsv + dcs[k, :, c]
-            lrow = jnp.broadcast_to(jnp.concatenate(lacc, axis=1), (8, di))
+            lrow = jnp.broadcast_to(jnp.concatenate(lacc, axis=1), (8, w))
             lhi, llo = two(lrow)
             lsum[k] = (dot_nt(lhi, e2[0:128, :]) + dot_nt(llo, e2[0:128, :]))[0:1]
-            ext[r, di : di + n] = gb * slope[r, di : di + n].astype(f32)
-            ext[r, di + n :] = gc * slope[r, di + n :].astype(f32)
+            if last_part:
+                ext[r, w : w + n] = (gb + dbp[r, :]) * slope2[r, :n].astype(f32)
+                ext[r, w + n :] = (gc + dcp[r, :]) * slope2[r, n:].astype(f32)
+            else:
+                dbp_o[r, :] = gb
+                dcp_o[r, :] = gc
 
         def strip(t, carry):
             r = pl.ds(pl.multiple_of(t * 16, 16), 16)
             re = pl.ds(pl.multiple_of(TB + t * 16, 16), 16)
-            x = xc[r, :].astype(f32)
+            x = x_in[r, :].astype(f32)
             es = sp[re, :] * sr[r, :]
             q = gxd[r, :].astype(f32) + es
             gx = sp[r, :] * q + dsk[...] * dy[r, :].astype(f32)
-            ext[r, 0:di] = gx * slope[r, 0:di].astype(f32)
+            ext[r, 0:w] = gx * slope[r, :].astype(f32)
             xq[r, :] = (x * q).astype(bf16)
             xe[r, :] = (x * es).astype(bf16)
             return carry
@@ -369,56 +383,61 @@
         et = dot_nt(xe[...], e2[0:128, :]) * dt
         ri = lax.broadcasted_iota(jnp.int32, (CH, CH), 0)
         ci = lax.broadcasted_iota(jnp.int32, (CH, CH), 1)
+        hl = lax.broadcasted_iota(jnp.int32, (1, 128), 1)
+        hm = ((hl >= h0) & (hl < h1)).astype(f32)
         tri = jnp.concatenate([(ci >= ri).astype(f32), (ci < ri).astype(f32)], axis=1)
         for k in range(nb):
             r = slice(k * CH, (k + 1) * CH)
-            v = jnp.concatenate([rk[r, :] + rin[r, :], et[r]], axis=0)
+            v = jnp.concatenate([rk[r, :] + rin[r, :] * hm, et[r]], axis=0)
             ga = jnp.dot(tri, v, precision=HIGH, preferred_element_type=f32) + lsum[k] * leaves[k]
-            dtk = dts[r, :128]
             ddt = (gdt[r] + ga * nr[...]) * dts[r, 128:]
-            gad = ga * dtk
+            gad = ga * dts[r, :128]
             acc_a, acc_d = gad[0:8], ddt[0:8]
             for q in range(8, CH, 8):
                 acc_a = acc_a + gad[q : q + 8]
                 acc_d = acc_d + ddt[q : q + 8]
             ga_o[...] += acc_a
             gdt_o[...] += acc_d
-            gp_o[r, conv:] = ddt.astype(bf16)
+            if last_part:
+                gp_o[r, cols:] = (ddt + ddtp[r, :]).astype(bf16)
+            else:
+                ddtp_o[r, :] = ddt
         for r0 in range(0, TB, 64):
-            for c0 in range(0, conv, 256):
+            rs = slice(r0, r0 + 64)
+            for c0 in range(0, cols, 256):
                 c = slice(c0, c0 + 256)
-                g0 = ext[r0 : r0 + 64, c]
-                xb = xbc[r0 : r0 + 64, c].astype(f32)
-                gsum = cw[3:4, c] * g0
+                g0 = ext[rs, c]
+                xb = pick(xbc, xbc2, rs, c0).astype(f32)
+                gsum = pick(cw, cw2, slice(3, 4), c0) * g0
                 ws = [None, None, None, g0 * xb]
                 for s in (1, 2, 3):
-                    gs = ext[r0 + s : r0 + s + 64, c] * tok[r0 : r0 + 64, 6 + s : 7 + s]
-                    gsum = gsum + cw[3 - s : 4 - s, c] * gs
+                    gs = ext[r0 + s : r0 + s + 64, c] * tok[rs, 6 + s : 7 + s]
+                    gsum = gsum + pick(cw, cw2, slice(3 - s, 4 - s), c0) * gs
                     ws[3 - s] = gs * xb
-                gp_o[r0 : r0 + 64, c] = gsum.astype(bf16)
+                gp_o[rs, c] = gsum.astype(bf16)
                 gb = g0[0:8]
                 for q in range(8, 64, 8):
                     gb = gb + g0[q : q + 8]
                 gb_o[:, c] += gb
                 for o in range(4):
-                    w = ws[o][0:8]
+                    v = ws[o][0:8]
                     for q in range(8, 64, 8):
-                        w = w + ws[o][q : q + 8]
-                    gw_o[8 * o : 8 * o + 8, c] += w
+                        v = v + ws[o][q : q + 8]
+                    gw_o[8 * o : 8 * o + 8, c] += v
         ext[TB : TB + 8, :] = ext[0:8, :]
 
         @pl.when(i == pl.num_programs(0) - 1)
         def _():
             zero = jnp.zeros((8, 256), f32)
-            for c0 in range(0, conv, 256):
+            for c0 in range(0, cols, 256):
                 c = slice(c0, c0 + 256)
-                xb = xbce[8:16, c].astype(f32)
+                xb = pick(xbce, xbce2, slice(8, 16), c0).astype(f32)
                 ext[8:16, c] = ext[TB : TB + 8, c]
                 ext[0:8, c] = zero
                 gsum = zero
                 for s in (1, 2, 3):
                     gs = ext[s : s + 8, c] * elink[:, 6 + s : 7 + s]
-                    gsum = gsum + cw[3 - s : 4 - s, c] * gs
+                    gsum = gsum + pick(cw, cw2, slice(3 - s, 4 - s), c0) * gs
                     gw_o[8 * (3 - s) : 8 * (3 - s) + 8, c] += gs * xb
                 edge_o[:, c] = jnp.concatenate([zero, gsum], axis=0).astype(bf16)
 
@@ -426,7 +445,7 @@
 
 
 def input_kernel(np_, di, conv, heads):
-    def kernel(ids, gpz, gpx, edge, u, e, *rest):
+    def kernel(ids, gpz, gpa, gpb, ea, eb, u, e, *rest):
         wz, wx = rest[:np_], rest[np_ : 2 * np_]
         gain, gi_o, gg_o, zbuf, xbuf = rest[2 * np_ :]
         i = pl.program_id(0)
@@ -438,9 +457,10 @@
             place(xbuf, ids, wx, conv + heads)
             gg_o[...] = jnp.zeros_like(gg_o)
 
-        gn = dot_nt(gpz[...], zbuf[...]) + dot_nt(gpx[...], xbuf[...])
+        wa = gpa.shape[1]
+        gn = dot_nt(gpz[...], zbuf[...]) + dot_nt(gpa[...], xbuf[:, :wa]) + dot_nt(gpb[...], xbuf[:, wa:])
         last = (i == pl.num_programs(0) - 1).astype(f32)
-        tail = dot_nt(edge[...], xbuf[:, :conv]) * last
+        tail = (dot_nt(ea[...], xbuf[:, :wa]) + dot_nt(eb[...], xbuf[:, wa:conv])) * last
         gn = jnp.concatenate([gn[: TB - 16], gn[TB - 16 :] + tail], axis=0)
         uf = u[...].astype(f32)
         scale = lax.rsqrt(jnp.mean(uf * uf, axis=-1, keepdims=True) + EPS)
@@ -470,6 +490,10 @@
     return [1 << k for k in reversed(range((n - 1).bit_length()))]
 
 
+def after(v, dep):
+    return lax.optimization_barrier((v, dep))[0]
+
+
 def gather_parts(v, axis):
     parts = [v]
     for bit in bits_of(lax.axis_size(axis)):
@@ -477,6 +501,19 @@
     return parts
 
 
+def in_order(parts, axis):
+    at = lax.axis_index(axis)
+    n = lax.axis_size(axis)
+    v = jnp.stack(parts)
+    rest = v.shape[1:]
+    bits = bits_of(n)
+    v = v.reshape((2,) * len(bits) + rest)
+    for k, bit in enumerate(reversed(bits)):
+        v = jnp.where((at // bit) % 2 == 0, v, jnp.flip(v, k))
+    order = tuple(reversed(range(len(bits))))
+    return v.transpose(order + tuple(range(len(bits), v.ndim))).reshape((n,) + rest)
+
+
 def part_ids(axis):
     ids = [lax.axis_index(axis)]
     for bit in bits_of(lax.axis_size(axis)):
@@ -484,32 +521,51 @@
     return ids
 
 
-def halve(v, axis, bit, at):
-    send = lax.dynamic_index_in_dim(v, 1 - at, 0, keepdims=False)
-    mine = lax.dynamic_index_in_dim(v, at, 0, keepdims=False)
-    got = swap(send, axis, bit)
-    return (mine.astype(f32) + got.astype(f32)).astype(bf16)
-
-
-def reduce_rows(g):
+def reduce_steps(gs):
     nw, ns = lax.axis_size("wshard"), lax.axis_size("seq")
     w, s = lax.axis_index("wshard"), lax.axis_index("seq")
-    cols = g.shape[1]
-    v = g.reshape(nw, -1, cols)
-    bit = 1
-    while bit < nw:
-        v = v.reshape(-1, 2, v.shape[-2], cols).swapaxes(0, 1)
-        v = halve(v, "wshard", bit, (w // bit) % 2)
-        bit *= 2
-    v = v.reshape(-1, cols)
-    n = v.shape[0]
-    for bit in [1 << k for k in range((ns - 1).bit_length())]:
-        v = halve(v.reshape(2, -1, cols), "seq", bit, (s // bit) % 2)
+    n = min(g.shape[0] for g in gs) // nw
+
+    def pick(at):
+        out = []
+        for g in gs:
+            v = g.reshape(nw // 2, 2, -1, g.shape[-1])
+            v = lax.dynamic_index_in_dim(v, at, 1, keepdims=False)
+            k = v.shape[1] // n
+            out += [v[:, q * n : (q + 1) * n] for q in range(k)]
+        return jnp.concatenate(out, axis=2) if len(out) > 1 else out[0]
+
+    def add(a, b):
+        return (a.astype(f32) + b.astype(f32)).astype(bf16)
+
+    steps = [("wshard", 1 << k) for k in range(1, (nw - 1).bit_length())]
+    steps += [("seq", 1 << k) for k in range((ns - 1).bit_length())]
+    send, keep = pick(1 - w % 2), pick(w % 2)
+    yield send
+    v = add(keep, swap(send, "wshard", 1))
+    for axis, bit in steps:
+        at = ((w if axis == "wshard" else s) // bit) % 2
+        if axis == "wshard":
+            v = v.reshape(-1, 2, n, v.shape[-1]).swapaxes(0, 1)
+        else:
+            v = v.reshape(2, -1, v.shape[-1])
+        send = lax.dynamic_index_in_dim(v, 1 - at, 0, keepdims=False)
+        keep = lax.dynamic_index_in_dim(v, at, 0, keepdims=False)
+        yield send
+        v = add(keep, swap(send, axis, bit))
     for bit in bits_of(ns):
+        yield v
         got = swap(v, "seq", bit)
         first = (s // bit) % 2 == 0
         v = jnp.concatenate([jnp.where(first, v, got), jnp.where(first, got, v)], axis=0)
-    return v.astype(f32)
+    yield v.astype(f32)
+
+
+def reduce_small(v):
+    for axis in ("wshard", "seq"):
+        for bit in reversed(bits_of(lax.axis_size(axis))):
+            v = v + swap(v, axis, bit)
+    return v
 
 
 def pack_state(decay, state):
@@ -521,9 +577,8 @@
     return v[n : n + 8].astype(f32)[:1] + v[n + 8 : n + 16].astype(f32)[:1], v[:n].astype(f32)
 
 
-def carried(decay, state, sign):
+def carried(decay, state, sign, tokens):
     n = state.shape[0]
-    tokens = carried_tokens[0]
     span = 1
     while span < -(-LONGEST // tokens):
         d, s = unpack_state(shift(pack_state(decay, state), "seq", sign * span), n)
@@ -531,9 +586,6 @@
         decay = decay * d
         span *= 2
     return shift(state.astype(bf16), "seq", sign)
-
-
-carried_tokens = [1024]
 
 
 def body(inputs, cotangent, lengths, in_proj, out_proj, conv_weight, conv_bias, a_log, d_skip,
@@ -549,23 +601,29 @@
     docs = lengths.shape[1]
     nt, nc, nb = t // TB, t // CH, TB // CH
     wide = conv + 128
-    carried_tokens[0] = t
     wx, wz = in_proj[:, di:], in_proj[:, :di]
+    pc = conv // nw
+    width = -(-max(pc, di // nw, 384) // 128) * 128
+
+    def line(*vs):
+        vs = [v if v.ndim == 2 else v[None] for v in vs]
+        vs = [jnp.pad(v, ((0, 0), (0, (width if k == len(vs) - 1 else 128 * (k + 1)) - 128 * k - v.shape[1])))
+              for k, v in enumerate(vs)]
+        return jnp.concatenate(vs, axis=1)
+
+    small = jnp.concatenate(
+        [line(conv_weight), line(conv_bias), line(gate_gain), line(norm_gain), line(a_log, d_skip, dt_bias)], axis=0)
+    small = in_order(gather_parts(small, "wshard"), "wshard").astype(f32)
     wx_parts = gather_parts(wx, "wshard")
-    wz_parts = gather_parts(wz, "wshard")
-    wo_parts = gather_parts(out_proj, "wshard")
+    wz_parts = gather_parts(after(wz, wx_parts[1]), "wshard")
+    wo_parts = gather_parts(after(out_proj, wx_parts[1]), "wshard")
     ids = jnp.stack(part_ids("wshard")).astype(jnp.int32)
-    small = jnp.concatenate(
-        [conv_weight.reshape(-1), conv_bias, a_log, d_skip, dt_bias, norm_gain, gate_gain]
-    )[None]
-    small = lax.all_gather(small, "wshard", axis=0, tiled=True).astype(f32)
-    sizes = [taps * conv // nw, conv // nw, heads // nw, heads // nw, heads // nw, d // nw, di // nw]
-    cut, off = [], 0
-    for k in sizes:
-        cut.append(small[:, off : off + k])
-        off += k
-    cw = cut[0].reshape(nw, taps, conv // nw).swapaxes(0, 1).reshape(taps, conv)
-    cb, log_rate, skip, dtb, gain_in, gain_gate = [v.reshape(1, -1) for v in cut[1:]]
+    hw = heads // nw
+    cw = small[:, :taps, :pc].swapaxes(0, 1).reshape(taps, conv)
+    cb = small[:, taps, :pc].reshape(1, conv)
+    gain_gate = small[:, taps + 1, : di // nw].reshape(1, di)
+    gain_in = small[:, taps + 2, : d // nw].reshape(1, d)
+    log_rate, skip, dtb = [small[:, taps + 3, 128 * k : 128 * k + hw].reshape(1, heads) for k in range(3)]
     rate = -jnp.exp(log_rate)
     pad = ((0, 0), (0, 128 - heads))
     nr = jnp.pad(rate, pad)
@@ -624,7 +682,7 @@
     (nrm, xbc, xc, slope, xd, dts, cc, ct, st, dbf, end, tot, nrme, xbce) = call(
         front_kernel(nw, di, conv, heads), (nt,), ins, outs, scratch, 15,
         [ids, u, ue, gain_in] + wx_parts + [cw, cb, dtb, nr2, tok, e2], "front")
-    incoming = carried(tot, end, 1)
+    incoming = carried(tot, end, 1, t)
 
     crow = pl.BlockSpec((32, CH), lambda i, s: (0, i))
     srow = pl.BlockSpec((1, CH), lambda i, s: (0, i))
@@ -659,78 +717,114 @@
     (mixed, gn, dz, dy, edy, e, sf, dcs, rin, g_gate, g_skip, reach) = call(
         gate_kernel(nw, di, d), (nt,), ins, outs, scratch, 25,
         [ids, nrm, yin, xc, xc, cc, tok, st, dbf, incoming, u, cot] + wz_parts + wo_parts + [gain_gate, dsk, e2], "gate")
-    gend = carried(tot, reach, -1)
+    gend = carried(tot, reach, -1, t)
 
     tn = (((0,), (0,)), ((), ()))
     gw_out = lax.dot_general(gn, e, tn, preferred_element_type=f32).astype(bf16)
     gw_z = lax.dot_general(nrm, dz, tn, preferred_element_type=f32).astype(bf16)
 
-    outs = [
-        (rows(CH, di), (t, di), bf16),
-        (rows(CH, n), (t, n), f32),
-        (rows(CH, n), (t, n), f32),
-        (rows(CH, 128), (t, 128), f32),
-    ]
-    (gxd, dbi, dci, rk) = call(
-        inner_back_kernel(heads, di), (nc,),
-        [bspec, cspec, rows(CH, di), rows(CH, di), rows(CH, 128), crow, rows(CH, 16), srow],
-        outs, [pltpu.VMEM((CH, CH), f32), pltpu.VMEM((128, CH), f32)], 20,
-        [ids, xc, xc, xd, dy, cc, ct, tok, segr], "inner_back")
+    oz = reduce_steps([gw_out, gw_z])
+    oz_out = next(oz)
+    hh, hw2 = heads // 2, di // 2
+
+    def half_inner(k, dep):
+        outs = [
+            (rows(CH, hw2), (t, hw2), bf16),
+            (rows(CH, n), (t, n), f32),
+            (rows(CH, n), (t, n), f32),
+            (rows(CH, 128), (t, 128), f32),
+        ]
+        return call(
+            inner_back_kernel(p, hh * k, hh * (k + 1)), (nc,),
+            [bspec, cspec, rows(CH, hw2, k), rows(CH, hw2, k), rows(CH, 128), crow, rows(CH, 16), srow],
+            outs, [pltpu.VMEM((128, CH), f32)], 12,
+            [ids, xc, xc, xd, after(dy, dep), cc, ct, tok, segr], "inner_back")
 
     def rev(block, width, col=0):
         return pl.BlockSpec((block, width), lambda i, s: (nt - 1 - i, col))
 
-    rblk = pl.BlockSpec((nb, n, di), lambda i, s: (nt - 1 - i, 0, 0))
-    ins = [rev(TB, di), rev(TB, n, di // n), rev(TB, conv), rev(TB, conv), whole((16, conv)), rev(TB, di),
-           rev(TB, 256), rev(TB, 128), rev(TB, 16), whole((8, 16)), rev(TB, di), rev(TB, n), rev(TB, n),
-           rev(TB, 128), rev(TB, 128), rev(TB, di), rev(TB, di), rblk, rblk, whole((n, di)),
-           whole((taps, conv)), whole((1, di)), whole((1, 128)), whole((256, di))]
-    outs = [
-        (rev(TB, wide), (t, wide), bf16),
-        (whole((16, conv)), (16, conv), bf16),
-        (whole((8 * taps, conv)), (8 * taps, conv), f32),
-        (whole((8, conv)), (8, conv), f32),
-        (whole((8, 128)), (8, 128), f32),
-        (whole((8, 128)), (8, 128), f32),
-    ]
-    scratch = [
-        pltpu.VMEM((n, di), f32),
-        pltpu.VMEM((2 * TB + 8 * nb, di), f32),
-        pltpu.VMEM((TB, di), f32),
-        pltpu.VMEM((TB + 8, conv), f32),
-        pltpu.VMEM((8, 128), bf16),
-        pltpu.VMEM((TB, di), bf16),
-        pltpu.VMEM((TB, di), bf16),
-    ]
-    (gpx, edge, g_cw, g_cb, g_a, g_dt) = call(
-        back_kernel(di, conv, heads), (nt,), ins, outs, scratch, 25,
-        [ids, xc, xc, slope, xbc, xbce, xd, dts, cc, tok, elink, gxd, dbi, dci, rk, rin, dy, edy, sf, dcs, gend,
-         cw, dsk, nr, e2], "back")
-
-    gw_x = lax.dot_general(nrm, gpx, tn, preferred_element_type=f32)
-    gw_e = lax.dot_general(nrme, edge, tn, preferred_element_type=f32)
-    gw_x = jnp.concatenate([gw_x[:, :conv] + gw_e, gw_x[:, conv : conv + heads]], axis=1).astype(bf16)
-    edge_in = shift(edge, "seq", -1)
-
-    ins = [rows(TB, di), rows(TB, wide), whole((16, conv)), rows(TB, d), rows(TB, d)]
+    def at(shape, col):
+        return pl.BlockSpec(shape, lambda i, s: (0, col))
+
+    def half_back(k, inner, dep, extra):
+        gxd, dbi, dci, rk = inner
+        last = k == 1
+        cols = hw2 + 2 * n if last else hw2
+        rblk = pl.BlockSpec((nb, n, hw2), lambda i, s: (nt - 1 - i, 0, k))
+        ins = [rev(TB, hw2, k), rev(TB, n, di // n), rev(TB, hw2, k), rev(TB, hw2, k), at((16, hw2), k),
+               rev(TB, hw2, k), rev(TB, 256), rev(TB, 128), rev(TB, 16), whole((8, 16)), rev(TB, hw2),
+               rev(TB, n), rev(TB, n), rev(TB, 128), rev(TB, 128), rev(TB, hw2, k), rev(TB, hw2, k), rblk, rblk,
+               at((n, hw2), k), at((taps, hw2), k), at((1, hw2), k), whole((1, 128)), at((256, hw2), k)]
+        args = [ids, xc, xc, slope, xbc, xbce, xd, dts, cc, tok, elink, after(gxd, dep), dbi, dci, rk, rin, dy,
+                edy, sf, dcs, gend, cw, dsk, nr, e2]
+        outs = [
+            (rev(TB, cols + 128 * last), (t, cols + 128 * last), bf16),
+            (whole((16, cols)), (16, cols), bf16),
+            (whole((8 * taps, cols)), (8 * taps, cols), f32),
+            (whole((8, cols)), (8, cols), f32),
+            (whole((8, 128)), (8, 128), f32),
+            (whole((8, 128)), (8, 128), f32),
+        ]
+        if last:
+            ins += [rev(TB, 2 * n, di // (2 * n)), rev(TB, 2 * n, di // (2 * n)), at((16, 2 * n), di // (2 * n)),
+                    at((taps, 2 * n), di // (2 * n)), rev(TB, n), rev(TB, n), rev(TB, 128)]
+            args += [slope, xbc, xbce, cw] + list(extra)
+        else:
+            outs += [(rev(TB, n), (t, n), f32), (rev(TB, n), (t, n), f32), (rev(TB, 128), (t, 128), f32)]
+        scratch = [
+            pltpu.VMEM((n, hw2), f32),
+            pltpu.VMEM((2 * TB + 8 * nb, hw2), f32),
+            pltpu.VMEM((TB, hw2), f32),
+            pltpu.VMEM((TB + 8, cols), f32),
+            pltpu.VMEM((TB, hw2), bf16),
+            pltpu.VMEM((TB, hw2), bf16),
+        ]
+        return call(back_kernel(hw2, n, hh * k, hh * (k + 1), last), (nt,), ins, outs, scratch, 15, args, "back")
+
+    in_a = half_inner(0, oz_out)
+    oz_out = next(oz, oz_out)
+    in_b = half_inner(1, (oz_out, in_a[0]))
+    (gpa, edge_a, gw_a, gb_a, ga_a, gdt_a, dbp, dcp, ddtp) = half_back(0, in_a, in_b[0], None)
+    oz_out = next(oz, oz_out)
+    (gpb, edge_b, gw_b, gb_b, ga_b, gdt_b) = half_back(1, in_b, (oz_out, gpa), (dbp, dcp, ddtp))
+    oz_out = next(oz, oz_out)
+
+    gw_xa = lax.dot_general(nrm, gpa, tn, preferred_element_type=f32)
+    gw_xa = (gw_xa + lax.dot_general(nrme, edge_a, tn, preferred_element_type=f32)).astype(bf16)
+    gw_xb = lax.dot_general(nrm, after(gpb, oz_out), tn, preferred_element_type=f32)
+    cb2 = conv - hw2
+    gw_xe = lax.dot_general(nrme, edge_b, tn, preferred_element_type=f32)
+    gw_xb = jnp.concatenate([gw_xb[:, :cb2] + gw_xe, gw_xb[:, cb2 : cb2 + heads]], axis=1).astype(bf16)
+    ea_in, eb_in = shift(edge_a, "seq", -1), shift(edge_b, "seq", -1)
+
+    ins = [rows(TB, di), rows(TB, hw2), rows(TB, wide - hw2), whole((16, hw2)), whole((16, cb2)), rows(TB, d), rows(TB, d)]
     ins += [whole(v.shape) for v in wz_parts + wx_parts] + [whole((1, d))]
     outs = [(rows(TB, d), (t, d), bf16), (whole((8, d)), (8, d), f32)]
+    x_chain = reduce_steps([gw_xa, gw_xb])
+    x_out = next(x_chain)
     (grad_input, g_gain) = call(
         input_kernel(nw, di, conv, heads), (nt,), ins, outs,
         [pltpu.VMEM((d, di), bf16), pltpu.VMEM((d, wide), bf16)], 12,
-        [ids, dz, gpx, edge_in, u, e] + wz_parts + wx_parts + [gain_in], "input")
-
-    r_out, r_z, r_x = reduce_rows(gw_out), reduce_rows(gw_z), reduce_rows(gw_x)
+        [ids, dz, after(gpa, x_out), gpb, ea_in, eb_in, u, e] + wz_parts + wx_parts + [gain_in], "input")
+    g_cw = jnp.concatenate([gw_a, gw_b], axis=1)
+    g_cb = jnp.concatenate([gb_a, gb_b], axis=1)
+    g_a, g_dt = ga_a + ga_b, gdt_a + gdt_b
+    next(x_chain)
+    x_out = next(x_chain)
+    r_oz, r_x = list(oz)[-1], list(x_chain)[-1]
+    k = r_oz.shape[1] - di
+    r_out = jnp.concatenate([r_oz[:, q * d : (q + 1) * d] for q in range(k // d)], axis=0)
+    r_z = r_oz[:, k:]
     parts = [
         g_cw.reshape(taps, 8, conv).sum(1).reshape(-1),
         g_cb.sum(0),
+        g_gain.sum(0),
+        g_gate.sum(0),
         g_a.sum(0)[:heads] * rate[0],
         g_skip.sum(0).reshape(heads, p).sum(1),
         g_dt.sum(0)[:heads],
-        g_gain.sum(0),
-        g_gate.sum(0),
     ]
-    total = lax.psum(jnp.concatenate(parts), ("seq", "wshard"))
+    total = reduce_small(after(jnp.concatenate(parts), x_out))
     w = lax.axis_index("wshard")
     res, off = [], 0
     for k, part in enumerate(parts):
@@ -739,6 +833,7 @@
         v = v.reshape(taps, conv) if k == 0 else v
         width = v.shape[-1] // nw
         res.append(lax.dynamic_slice_in_dim(v, w * width, width, axis=v.ndim - 1))
+    res = [res[k] for k in (0, 1, 4, 5, 6, 2, 3)]
     return (mixed[None], grad_input[None], jnp.concatenate([r_z, r_x], axis=1), r_out) + tuple(res)
 
 

time: 424 us -> 382 us (0.901)
  blocking collectives: 57.7 us -> 0 us
  waiting for transfers between devices: 71.8 us -> 98.7 us
  starting transfers between devices: 67.3 us -> 56.3 us
  Pallas kernels: 138 us -> 147 us
  local copies, waits for them, and re-layouts: 38 us -> 29.6 us
    psum x1 -> x0, blocking collectives: 45.6 us -> none  [body(): total = lax.psum(jnp.concatenate(parts), ('seq', 'wshard'))]
    ppermute x8 -> x9, waiting for transfers between devices: 7.42 us -> 27.6 us  [shift(): lax.ppermute(v, axis, [(k, k + steps) for k in range(n) if 0 <= k + steps...]
    unnamed x1 -> x0, blocking collectives: 12 us -> none
    ppermute x8 -> x9, starting transfers between devices: 34.1 us -> 24.4 us  [shift(): lax.ppermute(v, axis, [(k, k + steps) for k in range(n) if 0 <= k + steps...]
    pallas_call x6 -> x8, Pallas kernels: 138 us -> 147 us  [call(): pl.pallas_call(kernel, grid_spec=pltpu.PrefetchScalarGridSpec(num_scalar_...]
    ppermute x33, waiting for transfers between devices: 64.4 us -> 71.2 us  [swap(): lax.ppermute(v, axis, [(k, k ^ bit) for k in range(lax.axis_size(axis))])]
    concatenate x2, local copies, waits for them, and re-layouts: 5.58 us -> 0.11 us  [the longest x1 0.08 us: body(): total = reduce_small(after(jnp.concatenate(parts), x_out))]
    slice x5, local copies, waits for them, and re-layouts: 5.09 us -> 0.09 us  [body(): v = total[off:off + part.shape[0]]]
  transfers between devices with their start and end apart: 41 -> 42, of which waited for: 14 -> 18; matrix products, arithmetic and copies ran while one was open for 17% -> 12% of each run, Pallas kernels for 19% -> 24%
where the time goes in v2:
time: 382 us; the launch traced here: 375 us
  Pallas kernels  147 us (38%)
  waiting for transfers between devices  98.7 us (26%)
  starting transfers between devices  56.3 us (15%)
  local copies, waits for them, and re-layouts  29.6 us (8%)
  other arithmetic  27.2 us (7%)
  matrix products  13.6 us (4%)
    pallas_call x8, Pallas kernels, call(): pl.pallas_call(kernel, grid_spec=pltpu.PrefetchScalarGridSpec(num_scalar_...  147 us
    ppermute x33, waiting for transfers between devices, swap(): lax.ppermute(v, axis, [(k, k ^ bit) for k in range(lax.axis_size(axis))])  71.2 us
    ppermute x33, starting transfers between devices, swap(): lax.ppermute(v, axis, [(k, k ^ bit) for k in range(lax.axis_size(axis))])  31.9 us
    ppermute x9, waiting for transfers between devices, shift(): lax.ppermute(v, axis, [(k, k + steps) for k in range(n) if 0 <= k + steps...  27.6 us
    ppermute x9, starting transfers between devices, shift(): lax.ppermute(v, axis, [(k, k + steps) for k in range(n) if 0 <= k + steps...  24.4 us
    convert_element_type x10, other arithmetic, add(): return (a.astype(f32) + b.astype(f32)).astype(bf16)  7.64 us
  transfers between devices with their start and end apart: 42, of which 18 were waited for; matrix products, arithmetic and copies ran while one was open for 12% of the time, Pallas kernels for 24%

profile of v2, /device:TPU:0, one launch (start us, length us, event | category | flops | bytes accessed | tf_op | source)
XLA Modules:
  0.0 374.7 jit_solution(14749864927279282570)
XLA Ops:
  10.2 4.3 %collective-permute-start = (bf16[16,768]{1,0:T(8,128)(2,1)}, bf16[16,768]{1,0:T(8,128)(2,1)}, u32[]{:S(2)}, u32[]{:S(2)}) collective-permute-start(bf16[16,768]{1,0:T(8,128)(2,1)} %slice_bitcast_fusion.1), channel_id=1, source_target_pairs={{0,4},{4,8},{8,12},{12,16},{16,20},{20,24},{24,28},{1,5},{5,9},{9,... | collective-permute-start | bytes 73736 | tf_op jit(solution)/shard_map/ppermute | solution.py:486
  19.2 8.2 %collective-permute-done.4.rest_1_.rest_5_ = bf16[192,1816]{1,0:T(8,128)(2,1)S(1)} collective-permute-done((bf16[192,1816]{1,0:T(8,128)(2,1)S(1)}, bf16[192,1816]{1,0:T(8,128)(2,1)S(1)}, u32[]{:S(2)}, u32[]{:S(2)}) %collective-permute-start.4) | collective-permute-done | bytes 697376 | tf_op jit(solution)/shard_map/ppermute | solution.py:481
  32.6 20.5 %front.1 = (bf16[1024,768]{1,0:T(8,128)(2,1)}, bf16[1024,1792]{1,0:T(8,128)(2,1)}, bf16[1024,1792]{1,0:T(8,128)(2,1)}, bf16[1024,1792]{1,0:T(8,128)(2,1)}, bf16[...) custom-call(s32[4]{0:T(128)} %pad_add_fusion.ids, ...), custom_call_target="tpu_custom_call" | custom-call | flops 1650000000 | bytes 1048576 | tf_op jit(solution)/shard_map/front/pallas_call | solution.py:45
  62.0 6.7 %collective-permute-done.7 = bf16[144,1536]{1,0:T(8,128)(2,1)S(1)} collective-permute-done((bf16[144,1536]{1,0:T(8,128)(2,1)S(1)}, bf16[144,1536]{1,0:T(8,128)(2,1)S(1)}, u32[]{:S(2)}, u32[]{:S(2)}) %collective-permute-start.7) | collective-permute-done | bytes 442400 | tf_op jit(solution)/shard_map/ppermute | solution.py:486
  68.9 5.3 %collective-permute-start.8 = (bf16[144,1536]{1,0:T(8,128)(2,1)S(1)}, bf16[144,1536]{1,0:T(8,128)(2,1)S(1)}, u32[]{:S(2)}, u32[]{:S(2)}) collective-permute-start(bf16[144,1536]{1,0:T(8,128)(2,1)S(1)} %pad_maximum_fusion.9), channel_id=1, source_target_pairs={{0,8},{4,12},{8,16},{12,20},{16,24},{20,28},{1,9},{5,13},{9,17},{1... | collective-permute-start | bytes 1327112 | tf_op jit(solution)/shard_map/ppermute | solution.py:486
  76.1 11.9 %collective-permute-done.13.rest_5_ = bf16[384,768]{1,0:T(8,128)(2,1)} collective-permute-done((bf16[384,768]{1,0:T(8,128)(2,1)S(1)}, bf16[384,768]{1,0:T(8,128)(2,1)}, u32[]{:S(2)}, u32[]{:S(2)}) %collective-permute-start.13) | collective-permute-done | bytes 589856 | tf_op jit(solution)/shard_map/ppermute | solution.py:481
  89.0 4.3 %collective-permute-start.9 = (bf16[128,1536]{1,0:T(8,128)(2,1)}, bf16[128,1536]{1,0:T(8,128)(2,1)}, u32[]{:S(2)}, u32[]{:S(2)}) collective-permute-start(bf16[128,1536]{1,0:T(8,128)(2,1)} %add_convert_fusion.7), channel_id=1, source_target_pairs={{0,4},{4,8},{8,12},{12,16},{16,20},{20,24},{24,28},{1,5},{5,9},{9,... | collective-permute-start | bytes 1179656 | tf_op jit(solution)/shard_map/ppermute | solution.py:486
  95.4 10.1 %inner.1.yin = bf16[1024,1536]{1,0:T(8,128)(2,1)} custom-call(s32[4]{0:T(128)} %pad_add_fusion.ids, bf16[1024,1792]{1,0:T(8,128)(2,1)} %get-tuple-element.72.b.c.x.c_in.x_in.b_in, bf16[1024,1792]{1,0:T(8,128)(2,1)} %get-tuple-element.72.b.c.x.c_in.x_in.b_in, bf16[1024,1536]{1,0:T(8,128)(2,1)} %get-tuple-element.73.xd, f32[1024,128]{1,0:T(8,128)} %get-tuple-element.74.cc, ...), custom_call_target="tpu_custom_call" | custom-call | flops 1100000000 | bytes 1048576 | tf_op jit(solution)/shard_map/inner/pallas_call | solution.py:45
  106.6 37.5 %gate.1 = (bf16[1024,768]{1,0:T(8,128)(2,1)}, bf16[1024,1536]{1,0:T(8,128)(2,1)}, bf16[1024,1536]{1,0:T(8,128)(2,1)}, bf16[1024,1536]{1,0:T(8,128)(2,1)}, bf16[1...) custom-call(s32[4]{0:T(128)} %pad_add_fusion.ids, ...), custom_call_target="tpu_custom_call" | custom-call | flops 2750000128 | bytes 1048576 | tf_op jit(solution)/shard_map/gate/pallas_call | solution.py:45
  144.1 5.0 %convolution_convert_fusion.1 = bf16[1536,768]{1,0:T(8,128)(2,1)S(1)} fusion(bf16[1024,1536]{1,0:T(8,128)(2,1)} %get-tuple-element.89, bf16[1024,768]{1,0:T(8,128)(2,1)} %get-tuple-element.90.e), kind=kOutput, calls=%fused_computation.2 | convolution fusion | flops 2417098752 | bytes 7077888 | tf_op jit(solution)/shard_map/dot_general | solution.py:723
  159.1 12.8 %collective-permute-done.17 = bf16[144,1536]{1,0:T(8,128)(2,1)S(1)} collective-permute-done((bf16[144,1536]{1,0:T(8,128)(2,1)S(1)}, bf16[144,1536]{1,0:T(8,128)(2,1)S(1)}, u32[]{:S(2)}, u32[]{:S(2)}) %collective-permute-start.17) | collective-permute-done | bytes 442400 | tf_op jit(solution)/shard_map/ppermute | solution.py:486
  177.7 8.0 %collective-permute-done.18 = bf16[144,1536]{1,0:T(8,128)(2,1)S(1)} collective-permute-done((bf16[144,1536]{1,0:T(8,128)(2,1)S(1)}, bf16[144,1536]{1,0:T(8,128)(2,1)S(1)}, u32[]{:S(2)}, u32[]{:S(2)}) %collective-permute-start.18) | collective-permute-done | bytes 442400 | tf_op jit(solution)/shard_map/ppermute | solution.py:486
  191.1 13.6 %inner_back.2 = (bf16[1024,768]{1,0:T(8,128)(2,1)}, f32[1024,128]{1,0:T(8,128)}, f32[1024,128]{1,0:T(8,128)}, f32[1024,128]{1,0:T(8,128)}) custom-call(s32[4]{0:T(128)} %pad_add_fusion.ids, bf16[1024,1792]{1,0:T(8,128)(2,1)} %get-tuple-element.72.b.c.x.c_in.x_in.b_in, bf16[1024,1792]{1,0:T(8,128)(2,1)} %get-tuple-element.72.b.c.x.c_in.x_in.b_in, ...), custom_call_target="tpu_custom_call" | custom-call | flops 1320000000 | bytes 1048576 | tf_op jit(solution)/shard_map/inner_back/pallas_call | solution.py:45
  204.7 13.3 %inner_back.3 = (bf16[1024,768]{1,0:T(8,128)(2,1)}, f32[1024,128]{1,0:T(8,128)}, f32[1024,128]{1,0:T(8,128)}, f32[1024,128]{1,0:T(8,128)}) custom-call(s32[4]{0:T(128)} %pad_add_fusion.ids, bf16[1024,1792]{1,0:T(8,128)(2,1)} %get-tuple-element.72.b.c.x.c_in.x_in.b_in, bf16[1024,1792]{1,0:T(8,128)(2,1)} %get-tuple-element.72.b.c.x.c_in.x_in.b_in, ...), custom_call_target="tpu_custom_call" | custom-call | flops 1320000000 | bytes 1048576 | tf_op jit(solution)/shard_map/inner_back/pallas_call | solution.py:45
  218.8 17.7 %back.2 = (bf16[1024,768]{1,0:T(8,128)(2,1)}, bf16[16,768]{1,0:T(8,128)(2,1)}, f32[32,768]{1,0:T(8,128)}, f32[8,768]{1,0:T(8,128)}, f32[8,128]{1,0:T(8,128)}, /*...) custom-call(s32[4]{0:T(128)} %pad_add_fusion.ids, ...), custom_call_target="tpu_custom_call" | custom-call | flops 1650000000 | bytes 1048576 | tf_op jit(solution)/shard_map/back/pallas_call | solution.py:45
  246.8 18.8 %back.3 = (bf16[1024,1152]{1,0:T(8,128)(2,1)}, bf16[16,1024]{1,0:T(8,128)(2,1)}, f32[32,1024]{1,0:T(8,128)}, f32[8,1024]{1,0:T(8,128)}, f32[8,128]{1,0:T(8,128)}, /*index=5*/f32[8,128]{1,0:T(8,128)}) custom-call(s32[4]{0:T(128)} %pad_add_fusion.ids, bf16[1024,1792]{1,0:T(8,128)(2,1)} %get-tuple-element.72.b.c.x.c_in.x_in.b_in, ...), custom_call_target="tpu_custom_call" | custom-call | flops 1650000000 | bytes 1048576 | tf_op jit(solution)/shard_map/back/pallas_call | solution.py:45
  269.2 3.9 %collective-permute-start.24 = (bf16[48,3072]{1,0:T(8,128)(2,1)S(1)}, bf16[48,3072]{1,0:T(8,128)(2,1)S(1)}, u32[]{:S(2)}, u32[]{:S(2)}) collective-permute-start(bf16[48,3072]{1,0:T(8,128)(2,1)S(1)} %dynamic-slice_bitcast_fusion.8), channel_id=1, source_target_pairs={{0,8},{4,12},{8,0},{12,4},{16,24},{20,28},{24,16},{28,20},{1,9},{5... | collective-permute-start | bytes 884744 | tf_op jit(solution)/shard_map/ppermute | solution.py:481
  281.9 7.0 %collective-permute-done.25 = bf16[24,3072]{1,0:T(8,128)(2,1)S(1)} collective-permute-done((bf16[24,3072]{1,0:T(8,128)(2,1)S(1)}, bf16[24,3072]{1,0:T(8,128)(2,1)S(1)}, u32[]{:S(2)}, u32[]{:S(2)}) %collective-permute-start.25) | collective-permute-done | bytes 147488 | tf_op jit(solution)/shard_map/ppermute | solution.py:481
  291.5 5.9 %collective-permute-done.26 = bf16[24,3072]{1,0:T(8,128)(2,1)S(1)} collective-permute-done((bf16[24,3072]{1,0:T(8,128)(2,1)S(1)}, bf16[24,3072]{1,0:T(8,128)(2,1)S(1)}, u32[]{:S(2)}, u32[]{:S(2)}) %collective-permute-start.26) | collective-permute-done | bytes 147488 | tf_op jit(solution)/shard_map/ppermute | solution.py:481
  297.5 11.8 %collective-permute-done.30 = bf16[1,192,1816]{2,1,0:T(8,128)(2,1)S(1)} collective-permute-done((bf16[1,192,1816]{2,1,0:T(8,128)(2,1)S(1)}, bf16[1,192,1816]{2,1,0:T(8,128)(2,1)S(1)}, u32[]{:S(2)}, u32[]{:S(2)}) %collective-permute-start.30) | collective-permute-done | bytes 697376 | tf_op jit(solution)/shard_map/ppermute | solution.py:481
  312.4 7.8 %collective-permute-done.31 = bf16[96,1816]{1,0:T(8,128)(2,1)S(1)} collective-permute-done((bf16[96,1816]{1,0:T(8,128)(2,1)S(1)}, bf16[96,1816]{1,0:T(8,128)(2,1)S(1)}, u32[]{:S(2)}, u32[]{:S(2)}) %collective-permute-start.31) | collective-permute-done | bytes 348704 | tf_op jit(solution)/shard_map/ppermute | solution.py:481
  322.2 3.7 collective-permute-done.32
  329.4 15.4 %input.1 = (bf16[1024,768]{1,0:T(8,128)(2,1)}, f32[8,768]{1,0:T(8,128)}) custom-call(s32[4]{0:T(128)} %pad_add_fusion.ids, bf16[1024,1536]{1,0:T(8,128)(2,1)} %get-tuple-element.83.gpz, bf16[1024,768]{1,0:T(8,128)(2,1)} %get-tuple-element.117.gpa, bf16[1024,1152]{1,0:T(8,128)(2,1)} %get-tuple-element.115.gpb, bf16[16,768]{1,0:T(8,128)(2,1)} %collective-permute-done.22.ea, ...), custom_call_target="tpu_custom_call" | custom-call | flops 1320000000 | bytes 1048576 | tf_op jit(solution)/shard_map/input/pallas_call | solution.py:45
  356.5 5.0 %collective-permute-done.40 = f32[11336]{0:T(1024)S(1)} collective-permute-done((f32[11336]{0:T(1024)S(1)}, f32[11336]{0:T(1024)S(1)}, u32[]{:S(2)}, u32[]{:S(2)}) %collective-permute-start.40) | collective-permute-done | bytes 45376 | tf_op jit(solution)/shard_map/ppermute | solution.py:481
  (311 shorter events, 113.7 us)
Async XLA Ops:
  4.1 15.0 %collective-permute-start.2 = (bf16[8,512]{1,0:T(8,128)(2,1)S(1)}, bf16[8,512]{1,0:T(8,128)(2,1)S(1)}, u32[]{:S(2)}, u32[]{:S(2)}) collective-permute-start(bf16[8,512]{1,0:T(8,128)(2,1)S(1)} %concatenate.93), channel_id=1, source_target_pairs={{0,1},{1,0},{2,3},{3,2},{4,5},{5,4},{6,7},{7,6},{8,9},{9,8},{10,11... | collective-permute-start | bytes 24584 | tf_op jit(solution)/shard_map/ppermute | solution.py:481
  8.4 23.1 %collective-permute-start.5 = (bf16[192,1816]{1,0:T(8,128)(2,1)S(1)}, bf16[192,1816]{1,0:T(8,128)(2,1)S(1)}, u32[]{:S(2)}, u32[]{:S(2)}) collective-permute-start(bf16[192,1816]{1,0:T(8,128)(2,1)S(1)} %slice.181.rest_0_.rest_4_), channel_id=1, source_target_pairs={{0,1},{1,0},{2,3},{3,2},{4,5},{5,4},{6,7},{7,6},{8,9},{9,8},{10,11... | collective-permute-start | bytes 2092040 | tf_op jit(solution)/shard_map/ppermute | solution.py:481
  8.6 18.7 %collective-permute-start.4 = (bf16[192,1816]{1,0:T(8,128)(2,1)S(1)}, bf16[192,1816]{1,0:T(8,128)(2,1)S(1)}, u32[]{:S(2)}, u32[]{:S(2)}) collective-permute-start(bf16[192,1816]{1,0:T(8,128)(2,1)S(1)} %slice.181.rest_0_.rest_4_), channel_id=1, source_target_pairs={{0,2},{1,3},{2,0},{3,1},{4,6},{5,7},{6,4},{7,5},{8,10},{9,11},{10,... | collective-permute-start | bytes 2092040 | tf_op jit(solution)/shard_map/ppermute | solution.py:481
  10.2 21.2 %collective-permute-start = (bf16[16,768]{1,0:T(8,128)(2,1)}, bf16[16,768]{1,0:T(8,128)(2,1)}, u32[]{:S(2)}, u32[]{:S(2)}) collective-permute-start(bf16[16,768]{1,0:T(8,128)(2,1)} %slice_bitcast_fusion.1), channel_id=1, source_target_pairs={{0,4},{4,8},{8,12},{12,16},{16,20},{20,24},{24,28},{1,5},{5,9},{9,... | collective-permute-start | bytes 73736 | tf_op jit(solution)/shard_map/ppermute | solution.py:486
  59.9 16.2 %collective-permute-start.10 = (bf16[192,1536]{1,0:T(8,128)(2,1)S(1)}, bf16[192,1536]{1,0:T(8,128)(2,1)S(1)}, u32[]{:S(2)}, u32[]{:S(2)}) collective-permute-start(bf16[192,1536]{1,0:T(8,128)(2,1)S(1)} %slice.205.rest_0_), channel_id=1, source_target_pairs={{0,2},{1,3},{2,0},{3,1},{4,6},{5,7},{6,4},{7,5},{8,10},{9,11},{10,... | collective-permute-start | bytes 1769480 | tf_op jit(solution)/shard_map/ppermute | solution.py:481
  60.5 27.6 %collective-permute-start.13 = (bf16[384,768]{1,0:T(8,128)(2,1)S(1)}, bf16[384,768]{1,0:T(8,128)(2,1)}, u32[]{:S(2)}, u32[]{:S(2)}) collective-permute-start(bf16[384,768]{1,0:T(8,128)(2,1)S(1)} %copy-done.23), channel_id=1, source_target_pairs={{0,2},{1,3},{2,0},{3,1},{4,6},{5,7},{6,4},{7,5},{8,10},{9,11},{10,... | collective-permute-start | bytes 1769480 | tf_op jit(solution)/shard_map/ppermute | solution.py:481
  68.9 19.2 %collective-permute-start.8 = (bf16[144,1536]{1,0:T(8,128)(2,1)S(1)}, bf16[144,1536]{1,0:T(8,128)(2,1)S(1)}, u32[]{:S(2)}, u32[]{:S(2)}) collective-permute-start(bf16[144,1536]{1,0:T(8,128)(2,1)S(1)} %pad_maximum_fusion.9), channel_id=1, source_target_pairs={{0,8},{4,12},{8,16},{12,20},{16,24},{20,28},{1,9},{5,13},{9,17},{1... | collective-permute-start | bytes 1327112 | tf_op jit(solution)/shard_map/ppermute | solution.py:486
  74.3 31.2 %collective-permute-start.11 = (bf16[192,1536]{1,0:T(8,128)(2,1)S(1)}, bf16[192,1536]{1,0:T(8,128)(2,1)S(1)}, u32[]{:S(2)}, u32[]{:S(2)}) collective-permute-start(bf16[192,1536]{1,0:T(8,128)(2,1)S(1)} %slice.205.rest_0_), channel_id=1, source_target_pairs={{0,1},{1,0},{2,3},{3,2},{4,5},{5,4},{6,7},{7,6},{8,9},{9,8},{10,11... | collective-permute-start | bytes 1769480 | tf_op jit(solution)/shard_map/ppermute | solution.py:481
  74.4 31.2 %collective-permute-start.14 = (bf16[384,768]{1,0:T(8,128)(2,1)S(1)}, bf16[384,768]{1,0:T(8,128)(2,1)}, u32[]{:S(2)}, u32[]{:S(2)}) collective-permute-start(bf16[384,768]{1,0:T(8,128)(2,1)S(1)} %copy-done.23), channel_id=1, source_target_pairs={{0,1},{1,0},{2,3},{3,2},{4,5},{5,4},{6,7},{7,6},{8,9},{9,8},{10,11... | collective-permute-start | bytes 1769480 | tf_op jit(solution)/shard_map/ppermute | solution.py:481
  76.1 29.5 %collective-permute-start.12 = (bf16[192,1536]{1,0:T(8,128)(2,1)S(1)}, bf16[192,1536]{1,0:T(8,128)(2,1)S(1)}, u32[]{:S(2)}, u32[]{:S(2)}) collective-permute-start(bf16[192,1536]{1,0:T(8,128)(2,1)S(1)} %collective-permute-done.10.rest_1_), channel_id=1, source_target_pairs={{0,1},{1,0},{2,3},{3,2},{4,5},{5,4},{6,7},{7,6},{8,9},{9,8},{10,11... | collective-permute-start | bytes 1769480 | tf_op jit(solution)/shard_map/ppermute | solution.py:481
  88.1 17.5 %collective-permute-start.15 = (bf16[384,768]{1,0:T(8,128)(2,1)}, bf16[384,768]{1,0:T(8,128)(2,1)}, u32[]{:S(2)}, u32[]{:S(2)}) collective-permute-start(bf16[384,768]{1,0:T(8,128)(2,1)} %collective-permute-done.13.rest_5_), channel_id=1, source_target_pairs={{0,1},{1,0},{2,3},{3,2},{4,5},{5,4},{6,7},{7,6},{8,9},{9,8},{10,11... | collective-permute-start | bytes 1769480 | tf_op jit(solution)/shard_map/ppermute | solution.py:481
  89.0 16.6 %collective-permute-start.9 = (bf16[128,1536]{1,0:T(8,128)(2,1)}, bf16[128,1536]{1,0:T(8,128)(2,1)}, u32[]{:S(2)}, u32[]{:S(2)}) collective-permute-start(bf16[128,1536]{1,0:T(8,128)(2,1)} %add_convert_fusion.7), channel_id=1, source_target_pairs={{0,4},{4,8},{8,12},{12,16},{16,20},{20,24},{24,28},{1,5},{5,9},{9,... | collective-permute-start | bytes 1179656 | tf_op jit(solution)/shard_map/ppermute | solution.py:486
  157.4 16.1 %collective-permute-start.16 = (bf16[2,192,3072]{2,1,0:T(8,128)(2,1)}, bf16[2,192,3072]{2,1,0:T(8,128)(2,1)}, u32[]{:S(2)}, u32[]{:S(2)}) collective-permute-start(bf16[2,192,3072]{2,1,0:T(8,128)(2,1)} %pad_maximum_fusion.1), channel_id=1, source_target_pairs={{0,1},{1,0},{2,3},{3,2},{4,5},{5,4},{6,7},{7,6},{8,9},{9,8},{10,11... | collective-permute-start | bytes 7077896 | tf_op jit(solution)/shard_map/ppermute | solution.py:481
  157.7 14.3 %collective-permute-start.17 = (bf16[144,1536]{1,0:T(8,128)(2,1)S(1)}, bf16[144,1536]{1,0:T(8,128)(2,1)S(1)}, u32[]{:S(2)}, u32[]{:S(2)}) collective-permute-start(bf16[144,1536]{1,0:T(8,128)(2,1)S(1)} %pad_maximum_fusion.4), channel_id=1, source_target_pairs={{4,0},{8,4},{12,8},{16,12},{20,16},{24,20},{28,24},{5,1},{9,5},{13... | collective-permute-start | bytes 1327112 | tf_op jit(solution)/shard_map/ppermute | solution.py:486
  172.2 13.4 %collective-permute-start.18 = (bf16[144,1536]{1,0:T(8,128)(2,1)S(1)}, bf16[144,1536]{1,0:T(8,128)(2,1)S(1)}, u32[]{:S(2)}, u32[]{:S(2)}) collective-permute-start(bf16[144,1536]{1,0:T(8,128)(2,1)S(1)} %pad_maximum_fusion.10), channel_id=1, source_target_pairs={{8,0},{12,4},{16,8},{20,12},{24,16},{28,20},{9,1},{13,5},{17,9},{2... | collective-permute-start | bytes 1327112 | tf_op jit(solution)/shard_map/ppermute | solution.py:486
  177.1 62.0 %collective-permute-start.20 = (bf16[1,192,3072]{2,1,0:T(8,128)(2,1)}, bf16[1,192,3072]{2,1,0:T(8,128)(2,1)}, u32[]{:S(2)}, u32[]{:S(2)}) collective-permute-start(bf16[1,192,3072]{2,1,0:T(8,128)(2,1)} %constant_dynamic-slice_fusion.2), channel_id=1, source_target_pairs={{0,2},{1,3},{2,0},{3,1},{4,6},{5,7},{6,4},{7,5},{8,10},{9,11},{10,... | collective-permute-start | bytes 3538952 | tf_op jit(solution)/shard_map/ppermute | solution.py:481
  185.8 32.2 %collective-permute-start.19 = (bf16[128,1536]{1,0:T(8,128)(2,1)S(1)}, bf16[128,1536]{1,0:T(8,128)(2,1)S(1)}, u32[]{:S(2)}, u32[]{:S(2)}) collective-permute-start(bf16[128,1536]{1,0:T(8,128)(2,1)S(1)} %add_convert_fusion.6), channel_id=1, source_target_pairs={{4,0},{8,4},{12,8},{16,12},{20,16},{24,20},{28,24},{5,1},{9,5},{13... | collective-permute-start | bytes 1179656 | tf_op jit(solution)/shard_map/ppermute | solution.py:486
  236.5 92.9 %collective-permute-start.22 = (bf16[16,768]{1,0:T(8,128)(2,1)}, bf16[16,768]{1,0:T(8,128)(2,1)}, u32[]{:S(2)}, u32[]{:S(2)}) collective-permute-start(bf16[16,768]{1,0:T(8,128)(2,1)} %get-tuple-element.106), channel_id=1, source_target_pairs={{4,0},{8,4},{12,8},{16,12},{20,16},{24,20},{28,24},{5,1},{9,5},{13... | collective-permute-start | bytes 73736 | tf_op jit(solution)/shard_map/ppermute | solution.py:486
  241.0 27.0 %collective-permute-start.21 = (bf16[96,3072]{1,0:T(8,128)(2,1)S(1)}, bf16[96,3072]{1,0:T(8,128)(2,1)}, u32[]{:S(2)}, u32[]{:S(2)}) collective-permute-start(bf16[96,3072]{1,0:T(8,128)(2,1)S(1)} %dynamic-slice_bitcast_fusion.5), channel_id=1, source_target_pairs={{0,4},{4,0},{8,12},{12,8},{16,20},{20,16},{24,28},{28,24},{1,5},{5... | collective-permute-start | bytes 1769480 | tf_op jit(solution)/shard_map/ppermute | solution.py:481
  265.6 63.8 %collective-permute-start.23 = (bf16[16,1024]{1,0:T(8,128)(2,1)}, bf16[16,1024]{1,0:T(8,128)(2,1)}, u32[]{:S(2)}, u32[]{:S(2)}) collective-permute-start(bf16[16,1024]{1,0:T(8,128)(2,1)} %get-tuple-element.116), channel_id=1, source_target_pairs={{4,0},{8,4},{12,8},{16,12},{20,16},{24,20},{28,24},{5,1},{9,5},{13... | collective-permute-start | bytes 98312 | tf_op jit(solution)/shard_map/ppermute | solution.py:486
  290.9 18.5 %collective-permute-start.30 = (bf16[1,192,1816]{2,1,0:T(8,128)(2,1)S(1)}, bf16[1,192,1816]{2,1,0:T(8,128)(2,1)S(1)}, u32[]{:S(2)}, u32[]{:S(2)}) collective-permute-start(bf16[1,192,1816]{2,1,0:T(8,128)(2,1)S(1)} %constant_dynamic-slice_fusion.1), channel_id=1, source_target_pairs={{0,2},{1,3},{2,0},{3,1},{4,6},{5,7},{6,4},{7,5},{8,10},{9,11},{10,... | collective-permute-start | bytes 2092040 | tf_op jit(solution)/shard_map/ppermute | solution.py:481
  297.5 14.8 %collective-permute-start.27 = (bf16[48,3072]{1,0:T(8,128)(2,1)S(1)}, bf16[48,3072]{1,0:T(8,128)(2,1)S(1)}, u32[]{:S(2)}, u32[]{:S(2)}) collective-permute-start(bf16[48,3072]{1,0:T(8,128)(2,1)S(1)} %pad_maximum_fusion.12), channel_id=1, source_target_pairs={{0,8},{4,12},{8,0},{12,4},{16,24},{20,28},{24,16},{28,20},{1,9},{5... | collective-permute-start | bytes 884744 | tf_op jit(solution)/shard_map/ppermute | solution.py:481
  320.4 27.2 %collective-permute-start.28 = (bf16[96,3072]{1,0:T(8,128)(2,1)S(1)}, bf16[96,3072]{1,0:T(8,128)(2,1)S(1)}, u32[]{:S(2)}, u32[]{:S(2)}) collective-permute-start(bf16[96,3072]{1,0:T(8,128)(2,1)S(1)} %pad_maximum_fusion.8), channel_id=1, source_target_pairs={{0,4},{4,0},{8,12},{12,8},{16,20},{20,16},{24,28},{28,24},{1,5},{5... | collective-permute-start | bytes 1769480 | tf_op jit(solution)/shard_map/ppermute | solution.py:481
  326.0 21.5 %collective-permute-start.33 = (bf16[24,1816]{1,0:T(8,128)(2,1)S(1)}, bf16[24,1816]{1,0:T(8,128)(2,1)S(1)}, u32[]{:S(2)}, u32[]{:S(2)}) collective-permute-start(bf16[24,1816]{1,0:T(8,128)(2,1)S(1)} %dynamic-slice_bitcast_fusion.11), channel_id=1, source_target_pairs={{0,16},{4,20},{8,24},{12,28},{16,0},{20,4},{24,8},{28,12},{1,17},{... | collective-permute-start | bytes 261512 | tf_op jit(solution)/shard_map/ppermute | solution.py:481
  (58 other events, 561.8 us)
